TPU v7x, 32 devices: a whole 2x2x4 slice. The times are simulated.
32 devices in a mesh: dp: 16 (over z, y, core), tensor: 2 (over x).
Axes of the slice: x: 2, y: 2, z: 4, core: 2. Of those that a mesh axis runs over, the one named last changes fastest.
Arguments:
- tokens: bfloat16 [16384, 1024], P(('dp', 'tensor')), may hold values from -6 to 6
- segments: int32 [16, 1024], P('dp'), may hold values from 0 to 2, as said below
- w_qkv: bfloat16 [1024, 3072], P(None, 'tensor'), may hold values from -0.1875 to 0.1875
- b_qv: bfloat16 [2048], P('tensor'), may hold values from -3 to 3
- w_out: bfloat16 [1024, 1024], P('tensor'), may hold values from -0.75 to 0.75
- b_out: bfloat16 [1024], replicated, may hold values from -2 to 2
- w_up: bfloat16 [1024, 4096], P(None, 'tensor'), may hold values from -0.1875 to 0.1875
- b_up: bfloat16 [4096], P('tensor'), may hold values from -3 to 3
- w_down: bfloat16 [4096, 1024], P('tensor'), may hold values from -0.09375 to 0.09375
- b_down: bfloat16 [1024], replicated, may hold values from -2 to 2
- gain_one: bfloat16 [1024], replicated, may hold values from 0.099609375 to 1.8984375
- shift_one: bfloat16 [1024], replicated, may hold values from -2 to 2
- gain_two: bfloat16 [1024], replicated, may hold values from 0.099609375 to 1.8984375
- shift_two: bfloat16 [1024], replicated, may hold values from -2 to 2
- cotangent: bfloat16 [16384, 1024], P(('dp', 'tensor')), may hold values from -6 to 6
Outputs:
- layer_out: bfloat16 [16384, 1024], P(('dp', 'tensor'))
- input_grad: bfloat16 [16384, 1024], P(('dp', 'tensor'))
- grad_w_qkv: float32 [1024, 3072], P('dp', 'tensor')
- grad_b_qv: float32 [2048], P('tensor')
- grad_w_out: float32 [1024, 1024], P('tensor', 'dp')
- grad_b_out: float32 [1024], replicated
- grad_w_up: float32 [1024, 4096], P('dp', 'tensor')
- grad_b_up: float32 [4096], P('tensor')
- grad_w_down: float32 [4096, 1024], P('tensor', 'dp')
- grad_b_down: float32 [1024], replicated
- grad_gain_one: float32 [1024], replicated
- grad_shift_one: float32 [1024], replicated
- grad_gain_two: float32 [1024], replicated
- grad_shift_two: float32 [1024], replicated
Inputs may be any that keep to these rules, and one draw needn't show every extreme that they name: `segments`: along each sequence the numbers never fall.
All inputs are finite; a program needn't handle non-finite values.
Results may differ from a plain program's by a relative error of at most 0.02.
Values may be sent and summed in bfloat16 or wider, within the bound.
No kernel may reach another device: no remote copies, remote signals or barrier semaphores. Data moves between devices by JAX's collectives and lax.ppermute only.
A program may use at most 256 MiB of HBM per device.

v0:
```python
from functools import partial

import jax
import jax.numpy as jnp
from jax import lax
from jax.sharding import PartitionSpec as P

HEADS = 16
HEAD_DIM = 64


norm_eps = 1e-05
masked_fill = -1e30


def layer_norm(values, gain, shift):
    row_mean = jnp.mean(values, axis=-1, keepdims=True)
    centered = values - row_mean
    row_var = jnp.mean(centered * centered, axis=-1, keepdims=True)
    return centered * lax.rsqrt(row_var + norm_eps) * gain + shift


def contract_rows(left, right):
    return lax.dot_general(
        left, right, (((0,), (0,)), ((), ())), preferred_element_type=jnp.float32
    )


def contract_cols(left, right):
    return lax.dot_general(
        left, right, (((1,), (1,)), ((), ())), preferred_element_type=jnp.float32
    )


def spread_slots(local, rank, parts):
    slots = (lax.iota(jnp.int32, parts) == rank).astype(jnp.float32)
    return (slots[:, None] * local[None, :]).reshape(-1)


def masked_scores(query, keys, segment, first, slopes):
    scale = keys.shape[2] ** (-0.5)
    raw = jnp.einsum("qhd,khd->hqk", query, keys, preferred_element_type=jnp.float32) * scale
    rows_at = first + lax.iota(jnp.int32, query.shape[0])
    cols_at = lax.iota(jnp.int32, keys.shape[0])
    distance = (rows_at[:, None] - cols_at[None, :]).astype(jnp.float32)
    seg_rows = segment[first : first + query.shape[0]]
    allowed = (seg_rows[:, None] == segment[None, :]) & (distance >= 0)
    return jnp.where(allowed[None], raw - slopes[:, None, None] * distance[None], masked_fill)


def attend_forward(inputs, slopes, block):
    query, keys, values, segment = inputs
    outputs = []
    totals = []
    for first in range(0, keys.shape[0], block):
        scores = masked_scores(query[first : first + block], keys, segment, first, slopes)
        top = jnp.max(scores, axis=2, keepdims=True)
        log_total = top + jnp.log(jnp.sum(jnp.exp(scores - top), axis=2, keepdims=True))
        probs = jnp.exp(scores - log_total).astype(jnp.bfloat16)
        outputs.append(
            jnp.einsum("hqk,khd->qhd", probs, values, preferred_element_type=jnp.float32)
        )
        totals.append(log_total)
    return (jnp.concatenate(outputs, 0).astype(jnp.bfloat16), jnp.concatenate(totals, 1))


def attend_backward(inputs, slopes, block):
    query, keys, values, segment, log_total, grad_mixed = inputs
    scale = keys.shape[2] ** (-0.5)
    grad_keys = jnp.zeros(keys.shape, jnp.float32)
    grad_values = jnp.zeros(values.shape, jnp.float32)
    grad_query = []
    for first in range(0, keys.shape[0], block):
        rows = query[first : first + block]
        grad_rows = grad_mixed[first : first + block]
        scores = masked_scores(rows, keys, segment, first, slopes)
        probs = jnp.exp(scores - log_total[:, first : first + block])
        grad_probs = jnp.einsum(
            "qhd,khd->hqk", grad_rows, values, preferred_element_type=jnp.float32
        )
        inner = jnp.sum(probs * grad_probs, axis=2, keepdims=True)
        grad_scores = (probs * (grad_probs - inner)).astype(jnp.bfloat16)
        grad_query.append(
            jnp.einsum("hqk,khd->qhd", grad_scores, keys, preferred_element_type=jnp.float32)
            * scale
        )
        grad_keys = (
            grad_keys
            + jnp.einsum("hqk,qhd->khd", grad_scores, rows, preferred_element_type=jnp.float32)
            * scale
        )
        grad_values = grad_values + jnp.einsum(
            "hqk,qhd->khd",
            probs.astype(jnp.bfloat16),
            grad_rows,
            preferred_element_type=jnp.float32,
        )
    grad_query = jnp.concatenate(grad_query, 0)
    return jnp.stack((grad_query, grad_keys, grad_values), axis=2).astype(jnp.bfloat16)


def body(
    tokens,
    segments,
    w_qkv,
    b_qv,
    w_out,
    b_out,
    w_up,
    b_up,
    w_down,
    b_down,
    gain_one,
    shift_one,
    gain_two,
    shift_two,
    cotangent,
):
    rank = lax.axis_index("tensor")
    parts = lax.axis_size("tensor")
    count, length = segments.shape
    head_dim = HEAD_DIM
    local_heads = w_qkv.shape[1] // (3 * head_dim)
    block = length // 2
    rows_total = count * length
    local_rows = tokens.shape[0]
    head_index = rank * local_heads + lax.iota(jnp.int32, local_heads)
    slopes = 2.0 ** (-8.0 * (head_index + 1).astype(jnp.float32) / HEADS)
    gain_one_f = gain_one.astype(jnp.float32)
    shift_one_f = shift_one.astype(jnp.float32)
    gain_two_f = gain_two.astype(jnp.float32)
    shift_two_f = shift_two.astype(jnp.float32)
    source = tokens.astype(jnp.float32)
    normed_one = layer_norm(source, gain_one_f, shift_one_f).astype(jnp.bfloat16)
    rows_one = lax.all_gather(normed_one, "tensor", axis=0, tiled=True)
    joined = jnp.dot(rows_one, w_qkv, preferred_element_type=jnp.float32).reshape(
        count, length, local_heads, 3, head_dim
    )
    bias_pair = b_qv.astype(jnp.float32).reshape(local_heads, 2, head_dim)
    query = (joined[:, :, :, 0] + bias_pair[:, 0]).astype(jnp.bfloat16)
    keys = joined[:, :, :, 1].astype(jnp.bfloat16)
    values = (joined[:, :, :, 2] + bias_pair[:, 1]).astype(jnp.bfloat16)
    mixed, log_total = lax.map(
        partial(attend_forward, slopes=slopes, block=block), (query, keys, values, segments)
    )
    mixed = mixed.reshape(rows_total, local_heads * head_dim)
    attn_part = lax.psum_scatter(
        jnp.dot(
            lax.slice_in_dim(mixed, 0, local_rows * lax.axis_size("tensor"), axis=0),
            w_out,
            preferred_element_type=jnp.float32,
        ).astype(jnp.bfloat16),
        "tensor",
        scatter_dimension=0,
        tiled=True,
    ).astype(jnp.float32)
    resid = source + attn_part + b_out.astype(jnp.float32)
    normed_two = layer_norm(resid, gain_two_f, shift_two_f).astype(jnp.bfloat16)
    rows_two = lax.all_gather(normed_two, "tensor", axis=0, tiled=True)
    pre_act = jnp.dot(rows_two, w_up, preferred_element_type=jnp.float32) + b_up.astype(jnp.float32)
    hidden = jax.nn.gelu(pre_act, approximate=True).astype(jnp.bfloat16)
    mlp_part = lax.psum_scatter(
        jnp.dot(
            lax.slice_in_dim(hidden, 0, local_rows * lax.axis_size("tensor"), axis=0),
            w_down,
            preferred_element_type=jnp.float32,
        ).astype(jnp.bfloat16),
        "tensor",
        scatter_dimension=0,
        tiled=True,
    ).astype(jnp.float32)
    layer_out = resid + mlp_part + b_down.astype(jnp.float32)
    piece = lax.all_gather(cotangent, "tensor", axis=0, tiled=True)
    start = jnp.int32(0)
    grad_down = jnp.zeros((hidden.shape[1], cotangent.shape[1]), jnp.float32)
    grad_hidden = jnp.zeros(hidden.shape, jnp.float32)
    grad_down = grad_down + contract_rows(
        lax.dynamic_slice_in_dim(hidden, start, piece.shape[0], 0), piece
    )
    grad_hidden = lax.dynamic_update_slice_in_dim(
        grad_hidden, contract_cols(piece, w_down), start, 0
    )
    grad_down, grad_hidden = (grad_down, grad_hidden)
    unused, gelu_pull = jax.vjp(partial(jax.nn.gelu, approximate=True), pre_act)
    grad_pre = gelu_pull(grad_hidden)[0].astype(jnp.bfloat16)
    grad_up = contract_rows(rows_two, grad_pre)
    grad_b_up = jnp.sum(grad_pre.astype(jnp.float32), axis=0)
    grad_normed_two = lax.psum_scatter(
        contract_cols(
            lax.slice_in_dim(grad_pre, 0, local_rows * lax.axis_size("tensor"), axis=0), w_up
        ).astype(jnp.bfloat16),
        "tensor",
        scatter_dimension=0,
        tiled=True,
    ).astype(jnp.float32)
    unused, norm_two_pull = jax.vjp(layer_norm, resid, gain_two_f, shift_two_f)
    grad_resid_norm, grad_gain_two, grad_shift_two = norm_two_pull(grad_normed_two)
    seed = cotangent.astype(jnp.float32)
    grad_resid = seed + grad_resid_norm
    branch_grad = grad_resid.astype(jnp.bfloat16)
    piece = lax.all_gather(branch_grad, "tensor", axis=0, tiled=True)
    start = jnp.int32(0)
    grad_out = jnp.zeros((mixed.shape[1], branch_grad.shape[1]), jnp.float32)
    grad_mixed = jnp.zeros(mixed.shape, jnp.float32)
    grad_out = grad_out + contract_rows(
        lax.dynamic_slice_in_dim(mixed, start, piece.shape[0], 0), piece
    )
    grad_mixed = lax.dynamic_update_slice_in_dim(grad_mixed, contract_cols(piece, w_out), start, 0)
    grad_out, grad_mixed = (grad_out, grad_mixed)
    grad_mixed = grad_mixed.astype(jnp.bfloat16).reshape(count, length, local_heads, head_dim)
    grad_joined = lax.map(
        partial(attend_backward, slopes=slopes, block=block),
        (query, keys, values, segments, log_total, grad_mixed),
    )
    grad_joined = grad_joined.reshape(rows_total, local_heads, 3, head_dim)
    grad_b_qv = jnp.sum(grad_joined[:, :, 0::2].astype(jnp.float32), axis=0).reshape(-1)
    grad_joined = grad_joined.reshape(rows_total, local_heads * 3 * head_dim)
    grad_qkv = contract_rows(rows_one, grad_joined)
    grad_normed_one = lax.psum_scatter(
        contract_cols(
            lax.slice_in_dim(grad_joined, 0, local_rows * lax.axis_size("tensor"), axis=0), w_qkv
        ).astype(jnp.bfloat16),
        "tensor",
        scatter_dimension=0,
        tiled=True,
    ).astype(jnp.float32)
    unused, norm_one_pull = jax.vjp(layer_norm, source, gain_one_f, shift_one_f)
    grad_source, grad_gain_one, grad_shift_one = norm_one_pull(grad_normed_one)
    input_grad = (grad_resid + grad_source).astype(jnp.bfloat16)
    sum_qkv, sum_out, sum_up, sum_down = (
        lax.psum_scatter(
            grad_qkv.astype(jnp.bfloat16), "dp", scatter_dimension=0, tiled=True
        ).astype(jnp.float32),
        lax.psum_scatter(
            grad_out.astype(jnp.bfloat16), "dp", scatter_dimension=1, tiled=True
        ).astype(jnp.float32),
        lax.psum_scatter(
            grad_up.astype(jnp.bfloat16), "dp", scatter_dimension=0, tiled=True
        ).astype(jnp.float32),
        lax.psum_scatter(
            grad_down.astype(jnp.bfloat16), "dp", scatter_dimension=1, tiled=True
        ).astype(jnp.float32),
    )
    small = lax.psum(
        (
            grad_gain_one,
            grad_shift_one,
            jnp.sum(grad_resid, axis=0),
            grad_gain_two,
            grad_shift_two,
            jnp.sum(seed, axis=0),
            spread_slots(grad_b_qv, rank, parts),
            spread_slots(grad_b_up, rank, parts),
        ),
        ("dp", "tensor"),
    )
    qv_width = grad_b_qv.shape[0]
    up_width = grad_b_up.shape[0]
    sum_qv = lax.dynamic_slice_in_dim(small[6], rank * qv_width, qv_width)
    sum_bias_up = lax.dynamic_slice_in_dim(small[7], rank * up_width, up_width)
    return (
        layer_out.astype(jnp.bfloat16),
        input_grad,
        sum_qkv,
        sum_qv,
        sum_out,
        small[2],
        sum_up,
        sum_bias_up,
        sum_down,
        small[5],
        small[0],
        small[1],
        small[3],
        small[4],
    )


def solution(mesh):
    in_specs = (
        P(("dp", "tensor"), None),
        P("dp", None),
        P(None, "tensor"),
        P("tensor"),
        P("tensor", None),
        P(),
        P(None, "tensor"),
        P("tensor"),
        P("tensor", None),
        P(),
        P(),
        P(),
        P(),
        P(),
        P(("dp", "tensor"), None),
    )
    out_specs = (
        P(("dp", "tensor"), None),
        P(("dp", "tensor"), None),
        P("dp", "tensor"),
        P("tensor"),
        P("tensor", "dp"),
        P(),
        P("dp", "tensor"),
        P("tensor"),
        P("tensor", "dp"),
        P(),
        P(),
        P(),
        P(),
        P(),
    )
    return jax.shard_map(body, mesh=mesh, in_specs=in_specs, out_specs=out_specs, check_vma=False)
```

profile of v0, /device:TPU:0, one launch (start us, length us, event | category | flops | bytes accessed | tf_op | source)
XLA Modules:
  0.0 663.6 jit_solution(16148510106902534998)
XLA Ops:
  12.5 2.6 fusion.26
  20.6 30.5 %all-gather.5.cloned.1.call-done = bf16[1024,1024]{1,0:T(8,128)(2,1)} async-done(((bf16[512,1024]{1,0:T(8,128)(2,1)}), bf16[1024,1024]{1,0:T(8,128)(2,1)}) %all-gather.5.cloned.1.call-update) | async-done | bytes 2097168 | tf_op jit(solution)/shard_map/all_gather | solution.py:135
  51.1 5.2 fusion.68
  56.8 2.6 copy-done.14
  60.0 6.2 fusion.62
  66.2 3.5 exponential_reduce_fusion
  69.7 2.9 copy-done.1
  72.7 6.1 fusion.63
  78.8 3.7 exponential_reduce_fusion.1
  84.6 8.5 %fusion.47 = bf16[8,64,512]{2,1,0:T(8,128)(2,1)S(1)} fusion(bf16[1024,8,64]{0,2,1:T(8,128)(2,1)S(1)} %fusion.36, f32[8,512,1024]{2,1,0:T(8,128)} %copy-done.1, f32[8,512]{1,0:T(8,128)S(1)} %log_add_fusion), kind=kOutput, calls=%fused_computation.93 | convolution fusion | flops 545521664 | bytes 18366464 | tf_op jit(solution)/shard_map/while/body/eval_jaxpr/hqk,khd->qhd/dot_general | solution.py:61
  93.1 8.7 %fusion.44 = bf16[8,64,512]{2,1,0:T(8,128)(2,1)S(1)} fusion(bf16[1024,8,64]{0,2,1:T(8,128)(2,1)S(1)} %fusion.36, f32[8,512,1024]{2,1,0:T(8,128)} %copy-done.2, f32[8,512]{1,0:T(8,128)S(1)} %log_add_fusion.1), kind=kOutput, calls=%fused_computation.92 | convolution fusion | flops 545521664 | bytes 18366464 | tf_op jit(solution)/shard_map/while/body/eval_jaxpr/hqk,khd->qhd/dot_general | solution.py:61
  102.7 2.6 convolution_convert_fusion.6
  105.4 31.9 %reduce-scatter.9.cloned.1.call-done = bf16[512,1024]{1,0:T(8,128)(2,1)} async-done(((bf16[1024,1024]{1,0:T(8,128)(2,1)}), bf16[512,1024]{1,0:T(8,128)(2,1)}) %reduce-scatter.9.cloned.1.call-update) | async-done | bytes 1048592 | tf_op jit(solution)/shard_map/reduce_scatter | solution.py:147
  143.8 32.6 %all-gather.7.cloned.1.call-done = bf16[1024,1024]{1,0:T(8,128)(2,1)} async-done(((bf16[512,1024]{1,0:T(8,128)(2,1)}), bf16[1024,1024]{1,0:T(8,128)(2,1)}) %all-gather.7.cloned.1.call-update) | async-done | bytes 2097168 | tf_op jit(solution)/shard_map/all_gather | solution.py:159
  176.4 10.9 %fusion.69 = f32[1024,2048]{1,0:T(8,128)} fusion(bf16[1024,1024]{1,0:T(8,128)(2,1)} %all-gather.7.cloned.1.call-done, bf16[1024,2048]{1,0:T(8,128)(2,1)} %param.21), kind=kOutput, calls=%fused_computation.127 | convolution fusion | flops 4294967296 | bytes 14680064 | tf_op jit(solution)/shard_map/dot_general | solution.py:160
  187.3 23.7 %all-gather.9.cloned.1.call-done = bf16[1024,1024]{1,0:T(8,128)(2,1)} async-done(((bf16[512,1024]{1,0:T(8,128)(2,1)}), bf16[1024,1024]{1,0:T(8,128)(2,1)}) %all-gather.9.cloned.1.call-update) | async-done | bytes 2097168 | tf_op jit(solution)/shard_map/all_gather | solution.py:173
  211.0 13.7 %convert_reduce_fusion = (f32[2048]{0:T(1024)S(1)}, bf16[1024,2048]{1,0:T(8,128)(2,1)S(1)}) fusion(f32[1024,2048]{1,0:T(8,128)} %fusion.69, f32[2048]{0:T(1024)S(1)} %convert_element_type.225, bf16[1024,1024]{1,0:T(8,128)(2,1)} %all-gather.9.cloned.1.call-done, bf16[2048,1024]{1,0:T(8,128)(2,1)} %param.23), kind=kOutput, calls=%fused_computation.21 | convolution fusion | flops 4343199744 | bytes 18890752 | tf_op jit(solution)/shard_map/dot_general | solution.py:30
  226.7 5.8 convolution_convert_fusion.4
  232.6 11.3 %convolution_convert_fusion.5 = bf16[1024,1024]{1,0:T(8,128)(2,1)} fusion(bf16[2048,1024]{1,0:T(8,128)(2,1)} %param.23, f32[1024,2048]{1,0:T(8,128)} %fusion.69, f32[2048]{0:T(1024)S(1)} %convert_element_type.225), kind=kOutput, calls=%fused_computation.81 | convolution fusion | flops 4316987392 | bytes 14688256 | tf_op jit(solution)/shard_map/dot_general | solution.py:163
  244.1 20.4 %reduce-scatter.13.cloned.1.call-done = bf16[512,1024]{1,0:T(8,128)(2,1)} async-done(((bf16[1024,1024]{1,0:T(8,128)(2,1)}), bf16[512,1024]{1,0:T(8,128)(2,1)}) %reduce-scatter.13.cloned.1.call-update) | async-done | bytes 1048592 | tf_op jit(solution)/shard_map/reduce_scatter | solution.py:188
  264.5 2.9 convert_reduce_fusion.3
  268.8 29.6 %reduce-scatter.11.cloned.1.call-done = bf16[512,1024]{1,0:T(8,128)(2,1)} async-done(((bf16[1024,1024]{1,0:T(8,128)(2,1)}), bf16[512,1024]{1,0:T(8,128)(2,1)}) %reduce-scatter.11.cloned.1.call-update) | async-done | bytes 1048592 | tf_op jit(solution)/shard_map/reduce_scatter | solution.py:162
  298.4 4.0 fusion.58
  305.0 10.8 %convolution_convert_fusion.1 = bf16[2048,1024]{0,1:T(8,128)(2,1)} fusion(bf16[1024,1024]{1,0:T(8,128)(2,1)} %all-gather.9.cloned.1.call-done, f32[1024,2048]{1,0:T(8,128)} %fusion.69, f32[2048]{0:T(1024)S(1)} %convert_element_type.225), kind=kOutput, calls=%fused_computation.26 | convolution fusion | flops 4318035968 | bytes 14688256 | tf_op jit(solution)/shard_map/dot_general | solution.py:24
  315.9 9.5 %convolution_convert_fusion.2 = bf16[1024,2048]{1,0:T(8,128)(2,1)} fusion(bf16[1024,1024]{1,0:T(8,128)(2,1)} %all-gather.7.cloned.1.call-done, bf16[1024,2048]{1,0:T(8,128)(2,1)} %copy-done.49), kind=kOutput, calls=%fused_computation.27 | convolution fusion | flops 4297064448 | bytes 10485760 | tf_op jit(solution)/shard_map/dot_general | solution.py:24
  325.5 12.8 %all-gather.11.cloned.1.call-done = bf16[1024,1024]{1,0:T(8,128)(2,1)} async-done(((bf16[512,1024]{1,0:T(8,128)(2,1)}), bf16[1024,1024]{1,0:T(8,128)(2,1)}) %all-gather.11.cloned.1.call-update) | async-done | bytes 2097168 | tf_op jit(solution)/shard_map/all_gather | solution.py:201
  338.2 3.2 convolution_convert_fusion.8
  342.3 11.9 %multiply_reduce_fusion.1 = (f32[8,512]{1,0:T(8,128)S(1)}, f32[8,512,1024]{2,1,0:T(8,128)}) fusion(f32[8,512,1024]{2,1,0:T(8,128)} %copy-done.2, f32[8,512]{1,0:T(8,128)S(1)} %log_add_fusion.1, bf16[512,8,64]{0,2,1:T(8,128)(2,1)S(1)} %bitcast.107, bf16[1024,8,64]{0,2,1:T(8,128)(2,1)S(1)} %copy-done.9), kind=kOutput, calls=%fused_computation.3 | convolution fusion | flops 549449728 | bytes 35160064 | tf_op jit(solution)/shard_map/while/body/eval_jaxpr/qhd,khd->hqk/dot_general | solution.py:78
  354.2 13.1 %multiply_convert_fusion.1 = bf16[8,512,1024]{2,1,0:T(8,128)(2,1)S(1)} fusion(f32[8,512,1024]{2,1,0:T(8,128)} %get-tuple-element.100, f32[8,512,1024]{2,1,0:T(8,128)} %copy-done.2, f32[8,512]{1,0:T(8,128)S(1)} %get-tuple-element.99, f32[8,512]{1,0:T(8,128)S(1)} %log_add_fusion.1), kind=kLoop, calls=%fused_computation.2 | loop fusion | flops 16777216 | bytes 41975808 | tf_op jit(solution)/shard_map/while/body/eval_jaxpr/convert_element_type | solution.py:82
  367.3 2.9 fusion.51
  372.4 2.3 convolution_convert_fusion.7
  374.7 7.6 %fusion.42 = bf16[512,8,64]{0,2,1:T(8,128)(2,1)} fusion(bf16[8,512,1024]{2,1,0:T(8,128)(2,1)} %copy-done.5, f32[1,1024,8,3,64]{1,4,3,2,0:T(8,128)} %bitcast.105), kind=kOutput, calls=%fused_computation.90 | convolution fusion | flops 537395200 | bytes 9961472 | tf_op jit(solution)/shard_map/while/body/eval_jaxpr/hqk,khd->qhd/dot_general | solution.py:84
  382.3 13.2 %multiply_reduce_fusion = (f32[8,512]{1,0:T(8,128)S(1)}, f32[8,512,1024]{2,1,0:T(8,128)}) fusion(f32[8,512,1024]{2,1,0:T(8,128)} %copy-done.1, f32[8,512]{1,0:T(8,128)S(1)} %log_add_fusion, bf16[512,8,64]{0,2,1:T(8,128)(2,1)S(1)} %bitcast.109, bf16[1024,8,64]{0,2,1:T(8,128)(2,1)S(1)} %copy-done.10), kind=kOutput, calls=%fused_computation.1 | convolution fusion | flops 549449728 | bytes 35160064 | tf_op jit(solution)/shard_map/while/body/eval_jaxpr/qhd,khd->hqk/dot_general | solution.py:78
  395.4 15.9 %multiply_convert_fusion = bf16[8,512,1024]{2,1,0:T(8,128)(2,1)} fusion(f32[8,512,1024]{2,1,0:T(8,128)} %get-tuple-element.102, f32[8,512,1024]{2,1,0:T(8,128)} %copy-done.1, f32[8,512]{1,0:T(8,128)S(1)} %get-tuple-element.101, f32[8,512]{1,0:T(8,128)S(1)} %log_add_fusion), kind=kLoop, calls=%fused_computation | loop fusion | flops 16777216 | bytes 41975808 | tf_op jit(solution)/shard_map/while/body/eval_jaxpr/convert_element_type | solution.py:82
  411.3 7.5 %fusion.41 = bf16[512,8,64]{0,2,1:T(8,128)(2,1)} fusion(bf16[8,512,1024]{2,1,0:T(8,128)(2,1)} %multiply_convert_fusion, f32[1,1024,8,3,64]{1,4,3,2,0:T(8,128)} %bitcast.106), kind=kOutput, calls=%fused_computation.88 | convolution fusion | flops 537395200 | bytes 9961472 | tf_op jit(solution)/shard_map/while/body/eval_jaxpr/hqk,khd->qhd/dot_general | solution.py:84
  418.9 3.6 fusion.17
  422.5 9.3 %add_bitcast_fusion = bf16[1024,8,1,64]{0,3,1,2:T(8,128)(2,1)} fusion(f32[8,64,1024]{2,1,0:T(8,128)S(1)} %fusion.17, bf16[512,8,64]{0,2,1:T(8,128)(2,1)S(1)} %bitcast.108, f32[8,512,1024]{2,1,0:T(8,128)} %copy-done.2, f32[8,512]{1,0:T(8,128)S(1)} %log_add_fusion.1), kind=kOutput, calls=%fused_computation.70 | convolution fusion | flops 546308096 | bytes 20463616 | tf_op jit(solution)/shard_map/while/body/eval_jaxpr/hqk,qhd->khd/dot_general | solution.py:92
  434.0 5.6 multiply_bitcast_fusion
  443.4 4.7 convolution_convert_fusion.3
  448.2 7.6 %convolution_convert_fusion = bf16[1024,1536]{1,0:T(8,128)(2,1)} fusion(bf16[1024,1024]{1,0:T(8,128)(2,1)} %all-gather.5.cloned.1.call-done, bf16[1024,1536]{0,1:T(8,128)(2,1)} %bitcast.112), kind=kOutput, calls=%fused_computation.25 | convolution fusion | flops 3222798336 | bytes 8388608 | tf_op jit(solution)/shard_map/dot_general | solution.py:24
  459.9 30.6 %reduce-scatter.21.cloned.1.call-done = bf16[64,2048]{1,0:T(8,128)(2,1)} async-done(((bf16[1024,2048]{1,0:T(8,128)(2,1)}), bf16[64,2048]{1,0:T(8,128)(2,1)}) %reduce-scatter.21.cloned.1.call-update) | async-done | bytes 262160 | tf_op jit(solution)/shard_map/reduce_scatter | solution.py:237
  492.2 58.6 %reduce-scatter.19.cloned.1.call-done = bf16[512,64]{0,1:T(8,128)(2,1)} async-done(((bf16[512,1024]{0,1:T(8,128)(2,1)}), bf16[512,64]{0,1:T(8,128)(2,1)}) %reduce-scatter.19.cloned.1.call-update) | async-done | bytes 65552 | tf_op jit(solution)/shard_map/reduce_scatter | solution.py:234
  552.3 31.6 %reduce-scatter.15.cloned.1.call-done = bf16[512,1024]{1,0:T(8,128)(2,1)} async-done(((bf16[1024,1024]{1,0:T(8,128)(2,1)}), bf16[512,1024]{1,0:T(8,128)(2,1)}) %reduce-scatter.15.cloned.1.call-update) | async-done | bytes 1048592 | tf_op jit(solution)/shard_map/reduce_scatter | solution.py:219
  583.9 2.2 convert_reduce_fusion.2
  586.1 2.7 fusion.32
  588.8 41.7 %all-reduce = (f32[2048]{0:T(1024)S(1)}, f32[1024]{0:T(1024)}, f32[4096]{0:T(1024)S(1)}, f32[1024]{0:T(1024)}, f32[1024]{0:T(1024)}, /*index=5*/f32[1024]{0:T(1024)}, f32[1024]{0:T(1024)}, f32[1024]{0:T(1024)}) all-reduce(f32[2048]{0:T(1024)S(1)} %bitcast.118, ...), channel_id=1, replica_groups=mesh['dp'=16,'tensor'=2] {'dp','tensor'}, use_global_device_ids=true, to_apply=%region_20.21 | all-reduce | flops 12288 | bytes 98304 | tf_op jit(solution)/shard_map/psum | solution.py:244
  631.7 3.9 add_convert_fusion
  635.6 19.2 %reduce-scatter.17.cloned.1.call-done = bf16[64,1536]{1,0:T(8,128)(2,1)} async-done(((bf16[1024,1536]{1,0:T(8,128)(2,1)}), bf16[64,1536]{1,0:T(8,128)(2,1)}) %reduce-scatter.17.cloned.1.call-update) | async-done | bytes 196624 | tf_op jit(solution)/shard_map/reduce_scatter | solution.py:231
  (184 shorter events, 46.4 us)
Async XLA Ops:
  7.2 44.0 %copy-start = (bf16[1024,1536]{1,0:T(8,128)(2,1)S(1)}, bf16[1024,1536]{1,0:T(8,128)(2,1)}, u32[]{:S(2)}) copy-start(bf16[1024,1536]{1,0:T(8,128)(2,1)} %param.17) | copy-start | bytes 9437188
  7.2 8.0 %copy-start.41 = (bf16[1024]{0:T(1024)(128)(2,1)S(1)}, bf16[1024]{0:T(1024)(128)(2,1)}, u32[]{:S(2)}) copy-start(bf16[1024]{0:T(1024)(128)(2,1)} %param.18) | copy-start | bytes 6148
  7.2 43.9 %all-gather.5.cloned.1.call-start = ((), (), s32[]{:S(2)}) async-start(), calls=%async_computation.8 | async-start | bytes 3145728 | tf_op jit(solution)/shard_map/all_gather | solution.py:135
  8.8 3.6 copy-start.33
  8.9 8.1 %copy-start.39 = (s32[1,1024]{1,0:T(1,128)S(1)}, s32[1,1024]{1,0:T(1,128)}, u32[]{:S(2)}) copy-start(s32[1,1024]{1,0:T(1,128)} %param.16) | copy-start | bytes 12292
  15.2 122.1 %reduce-scatter.9.cloned.1.call-start = ((), (), s32[]{:S(2)}) async-start(), calls=%async_computation.9 | async-start | bytes 3145728 | tf_op jit(solution)/shard_map/reduce_scatter | solution.py:147
  56.4 3.6 copy-start.26
  56.6 16.1 %copy-start.16 = (bf16[1,1024,8,64]{1,3,2,0:T(8,128)(2,1)}, bf16[1,1024,8,64]{1,3,2,0:T(8,128)(2,1)S(1)}, u32[]{:S(2)}) copy-start(bf16[1,1024,8,64]{1,3,2,0:T(8,128)(2,1)S(1)} %fusion.34) | copy-start | bytes 3145732
  59.4 33.7 %copy-start.8 = (bf16[1024,8,64]{0,2,1:T(8,128)(2,1)}, bf16[1024,8,64]{0,2,1:T(8,128)(2,1)S(1)}, u32[]{:S(2)}) copy-start(bf16[1024,8,64]{0,2,1:T(8,128)(2,1)S(1)} %fusion.36) | copy-start | bytes 3145732
  66.2 6.5 copy-start.1
  66.2 6.5 copy-start.24
  66.2 6.5 copy-start.25
  78.8 5.7 copy-start.2
  93.1 8.7 %copy-start.27 = (bf16[8,64,512]{2,1,0:T(8,128)(2,1)}, bf16[8,64,512]{2,1,0:T(8,128)(2,1)S(1)}, u32[]{:S(2)}) copy-start(bf16[8,64,512]{2,1,0:T(8,128)(2,1)S(1)} %fusion.47) | copy-start | bytes 1572868
  93.1 9.6 %copy-start.48 = (bf16[512,1024]{1,0:T(8,128)(2,1)S(1)}, bf16[512,1024]{1,0:T(8,128)(2,1)}, u32[]{:S(2)}) copy-start(bf16[512,1024]{1,0:T(8,128)(2,1)} %param.19) | copy-start | bytes 3145732
  105.3 71.1 %all-gather.7.cloned.1.call-start = ((), (), s32[]{:S(2)}) async-start(), calls=%async_computation.10 | async-start | bytes 3145728 | tf_op jit(solution)/shard_map/all_gather | solution.py:159
  137.3 4.2 copy-start.3
  137.3 4.3 copy-start.6
  143.1 67.9 %all-gather.9.cloned.1.call-start = ((), (), s32[]{:S(2)}) async-start(), calls=%async_computation.12 | async-start | bytes 3145728 | tf_op jit(solution)/shard_map/all_gather | solution.py:173
  143.7 120.8 %reduce-scatter.13.cloned.1.call-start = ((), (), s32[]{:S(2)}) async-start(), calls=%async_computation.13 | async-start | bytes 3145728 | tf_op jit(solution)/shard_map/reduce_scatter | solution.py:188
  211.0 15.6 %copy-start.46 = (bf16[1024,2048]{1,0:T(8,128)(2,1)S(1)}, bf16[1024,2048]{1,0:T(8,128)(2,1)}, u32[]{:S(2)}) copy-start(bf16[1024,2048]{1,0:T(8,128)(2,1)} %param.21) | copy-start | bytes 12582916
  232.5 11.6 %copy-start.45 = (bf16[1024]{0:T(1024)(128)(2,1)S(1)}, bf16[1024]{0:T(1024)(128)(2,1)}, u32[]{:S(2)}) copy-start(bf16[1024]{0:T(1024)(128)(2,1)} %param.24) | copy-start | bytes 6148
  232.5 65.9 %reduce-scatter.11.cloned.1.call-start = ((), (), s32[]{:S(2)}) async-start(), calls=%async_computation.11 | async-start | bytes 3145728 | tf_op jit(solution)/shard_map/reduce_scatter | solution.py:162
  243.9 94.3 %all-gather.11.cloned.1.call-start = ((), (), s32[]{:S(2)}) async-start(), calls=%async_computation.14 | async-start | bytes 3145728 | tf_op jit(solution)/shard_map/all_gather | solution.py:201
  305.0 153.1 %reduce-scatter.23.cloned.1.call-start = ((), (), s32[]{:S(2)}) async-start(), calls=%async_computation.19 | async-start | bytes 4456448 | tf_op jit(solution)/shard_map/reduce_scatter | solution.py:240
  315.9 174.5 %reduce-scatter.21.cloned.1.call-start = ((), (), s32[]{:S(2)}) async-start(), calls=%async_computation.18 | async-start | bytes 4456448 | tf_op jit(solution)/shard_map/reduce_scatter | solution.py:237
  325.4 225.3 %reduce-scatter.19.cloned.1.call-start = ((), (), s32[]{:S(2)}) async-start(), calls=%async_computation.17 | async-start | bytes 1114112 | tf_op jit(solution)/shard_map/reduce_scatter | solution.py:234
  338.2 4.1 copy-start.9
  342.3 11.9 %copy-start.18 = (bf16[512,512]{0,1:T(8,128)(2,1)}, bf16[512,512]{0,1:T(8,128)(2,1)S(1)}, u32[]{:S(2)}) copy-start(bf16[512,512]{0,1:T(8,128)(2,1)S(1)} %get-tuple-element.87) | copy-start | bytes 1572868
  354.2 13.1 %copy-start.17 = (bf16[1,1024,8,64]{1,3,2,0:T(8,128)(2,1)S(1)}, bf16[1,1024,8,64]{1,3,2,0:T(8,128)(2,1)}, u32[]{:S(2)}) copy-start(bf16[1,1024,8,64]{1,3,2,0:T(8,128)(2,1)} %copy-done.16) | copy-start | bytes 3145732
  367.3 5.1 copy-start.5
  367.3 5.1 copy-start.28
  367.3 5.1 copy-start.30
  367.3 5.1 copy-start.47
  374.6 7.6 %copy-start.10 = (bf16[1024,8,64]{0,2,1:T(8,128)(2,1)S(1)}, bf16[1024,8,64]{0,2,1:T(8,128)(2,1)}, u32[]{:S(2)}) copy-start(bf16[1024,8,64]{0,2,1:T(8,128)(2,1)} %copy-done.8) | copy-start | bytes 3145732
  374.6 7.6 %copy-start.20 = (bf16[512,512]{0,1:T(8,128)(2,1)S(1)}, bf16[512,512]{0,1:T(8,128)(2,1)}, u32[]{:S(2)}) copy-start(bf16[512,512]{0,1:T(8,128)(2,1)} %get-tuple-element.88) | copy-start | bytes 1572868
  382.2 36.6 %slice-start = ((s8[16777216]{0:T(1024)(128)(4,1)}), s8[4194304]{0:T(1024)(128)(4,1)S(1)}, s32[]{:S(2)}) async-start(s8[16777216]{0:T(1024)(128)(4,1)} %bitcast.99), calls=%async_computation.20 | async-start | bytes 8388608
  382.2 36.6 %slice-start.1 = ((s8[16777216]{0:T(1024)(128)(4,1)}), s8[4194304]{0:T(1024)(128)(4,1)S(1)}, s32[]{:S(2)}) async-start(s8[16777216]{0:T(1024)(128)(4,1)} %bitcast.99), calls=%async_computation.21 | async-start | bytes 8388608
  395.4 23.5 %slice-start.2 = ((s8[16777216]{0:T(1024)(128)(4,1)}), s8[4194304]{0:T(1024)(128)(4,1)S(1)}, s32[]{:S(2)}) async-start(s8[16777216]{0:T(1024)(128)(4,1)} %bitcast.99), calls=%async_computation.22 | async-start | bytes 8388608
  395.4 23.5 %slice-start.3 = ((s8[16777216]{0:T(1024)(128)(4,1)}), s8[4194304]{0:T(1024)(128)(4,1)S(1)}, s32[]{:S(2)}) async-start(s8[16777216]{0:T(1024)(128)(4,1)} %bitcast.99), calls=%async_computation.23 | async-start | bytes 8388608
  418.9 3.6 copy-start.19
  431.9 152.0 %reduce-scatter.15.cloned.1.call-start = ((), (), s32[]{:S(2)}) async-start(), calls=%async_computation.15 | async-start | bytes 3145728 | tf_op jit(solution)/shard_map/reduce_scatter | solution.py:219
  434.0 5.6 copy-start.21
  448.1 206.7 %reduce-scatter.17.cloned.1.call-start = ((), (), s32[]{:S(2)}) async-start(), calls=%async_computation.16 | async-start | bytes 3342336 | tf_op jit(solution)/shard_map/reduce_scatter | solution.py:231
  455.8 128.1 %copy-start.32 = (f32[1024]{0:T(1024)S(1)}, f32[1024]{0:T(1024)}, u32[]{:S(2)}) copy-start(f32[1024]{0:T(1024)} %copy-done.31) | copy-start | bytes 12292
  455.8 128.1 %copy-start.34 = (f32[512]{0:T(512)S(1)}, f32[512]{0:T(512)}, u32[]{:S(2)}) copy-start(f32[512]{0:T(512)} %copy-done.33) | copy-start | bytes 6148
  455.8 130.2 %copy-start.38 = (f32[512]{0:T(512)S(1)}, f32[512]{0:T(512)}, u32[]{:S(2)}) copy-start(f32[512]{0:T(512)} %copy-done.37) | copy-start | bytes 6148
  455.8 130.3 %copy-start.36 = (f32[512]{0:T(512)S(1)}, f32[512]{0:T(512)}, u32[]{:S(2)}) copy-start(f32[512]{0:T(512)} %copy-done.35) | copy-start | bytes 6148
  (18 other events, 37.6 us)
Sparse Core Ops, SparseCore 0:
  15.3 35.8 all-gather.4
  105.4 31.8 reduce-scatter.8
  143.2 33.1 all-gather.6
  177.9 33.1 all-gather.8
  232.6 31.8 reduce-scatter.12
  266.6 31.8 reduce-scatter.10
  305.1 33.0 all-gather.10
  342.6 72.4 reduce-scatter.22
  418.9 71.4 reduce-scatter.20
  494.3 56.3 reduce-scatter.18
  553.0 30.8 reduce-scatter.14
  588.0 66.7 reduce-scatter.16
where the time goes:
time: 673 us; the launch traced here: 664 us
  waiting for transfers between devices  322 us (48%)
  matrix products  179 us (27%)
  other arithmetic  84 us (12%)
  blocking collectives  41.7 us (6%)
  local copies, waits for them, and re-layouts  21.2 us (3%)
  between operations  15.1 us (2%)
    reduce_scatter x1, waiting for transfers between devices, body(): lax.psum_scatter(grad_out.astype(jnp.bfloat16), 'dp', scatter_dimension=1...  58.6 us
    psum x1, blocking collectives, body(): lax.psum((grad_gain_one, grad_shift_one, jnp.sum(grad_resid, axis=0), gra...  41.7 us
    all_gather x1, waiting for transfers between devices, body(): rows_two = lax.all_gather(normed_two, 'tensor', axis=0, tiled=True)  32.6 us
    reduce_scatter x1, waiting for transfers between devices, body(): lax.psum_scatter(jnp.dot(lax.slice_in_dim(mixed, 0, local_rows * lax.axis...  31.9 us
    reduce_scatter x1, waiting for transfers between devices, body(): lax.psum_scatter(contract_cols(lax.slice_in_dim(grad_joined, 0, local_row...  31.6 us
    reduce_scatter x1, waiting for transfers between devices, body(): lax.psum_scatter(grad_up.astype(jnp.bfloat16), 'dp', scatter_dimension=0,...  30.6 us
    all_gather x1, waiting for transfers between devices, body(): rows_one = lax.all_gather(normed_one, 'tensor', axis=0, tiled=True)  30.5 us
    dot_general x4, matrix products, contract_rows(): lax.dot_general(left, right, (((0,), (0,)), ((), ())), preferred_element_...  30.2 us
  transfers between devices with their start and end apart: 12, of which 11 were waited for; matrix products, arithmetic and copies ran while one was open for 27% of the time, Pallas kernels for 0%

commit v1 on v0

--- a/solution.py
+++ b/solution.py
@@ -3,6 +3,8 @@
 import jax
 import jax.numpy as jnp
 from jax import lax
+from jax.experimental import pallas as pl
+from jax.experimental.pallas import tpu as pltpu
 from jax.sharding import PartitionSpec as P
 
 HEADS = 16
@@ -276,6 +278,522 @@
     )
 
 
+PIECE = 256
+
+
+def core_of(index):
+    return index % 2
+
+
+def swap_pairs():
+    return [((2 * k + c) * 2 + x, (2 * k + x) * 2 + c) for k in range(8) for c in (0, 1) for x in (0, 1)]
+
+
+def swap_only_pairs():
+    return [(a, b) for a, b in swap_pairs() if a != b]
+
+
+def flip_pairs(bit):
+    return [(d, d ^ bit) for d in range(16)]
+
+
+def flip_far_pairs(bit):
+    return [((d * 2 + x), (d ^ bit) * 2 + x) for d in range(16) for x in (0, 1) if d % 2 != x]
+
+
+def swap(value):
+    return lax.ppermute(value, ("dp", "tensor"), swap_pairs())
+
+
+def swap_far(value):
+    return lax.ppermute(value, ("dp", "tensor"), swap_only_pairs())
+
+
+def flip(value, bit):
+    return lax.ppermute(value, "dp", flip_pairs(bit))
+
+
+def flip_far(value, bit):
+    return lax.ppermute(value, ("dp", "tensor"), flip_far_pairs(bit))
+
+
+def after(value, *earlier):
+    return lax.optimization_barrier((value, *earlier))[0]
+
+
+def nt(left, right):
+    return lax.dot_general(
+        left, right, (((1,), (1,)), ((), ())), preferred_element_type=jnp.float32
+    )
+
+
+def nn(left, right):
+    return lax.dot_general(
+        left, right, (((1,), (0,)), ((), ())), preferred_element_type=jnp.float32
+    )
+
+
+def tn(left, right):
+    return lax.dot_general(
+        left, right, (((0,), (0,)), ((), ())), preferred_element_type=jnp.float32
+    )
+
+
+def both_halves(ref, core, lanes):
+    return jnp.concatenate([ref[core, :, lanes], ref[1 - core, :, lanes]], axis=0)
+
+
+def scores_of(keys, rows, slope, seg_col, seg_row, first, size):
+    part = nt(keys, rows)
+    place = lax.broadcasted_iota(jnp.int32, (keys.shape[0], 1), 0)
+    part = part + (place - first).astype(jnp.float32) * slope
+    same = seg_col[: keys.shape[0]] == seg_row
+    shape = (size, size)
+    ahead = lax.broadcasted_iota(jnp.int32, shape, 0) <= lax.broadcasted_iota(jnp.int32, shape, 1)
+    diag = jnp.where(same[first:] & ahead, part[first:], masked_fill)
+    if first == 0:
+        return [diag]
+    return [jnp.where(same[:first], part[:first], masked_fill), diag]
+
+
+def attend_kernel(core_ref, slope_ref, qkv_ref, col_ref, row_ref, mixed_ref, total_ref):
+    pair = pl.program_id(0)
+    core = core_ref[0]
+    half = qkv_ref.shape[1]
+    length = 2 * half
+    size = min(PIECE, half)
+    seg_col = col_ref[...]
+    for head in range(2):
+        at = head * 3 * HEAD_DIM
+        keys = both_halves(qkv_ref, core, slice(at + HEAD_DIM, at + 2 * HEAD_DIM))
+        values = both_halves(qkv_ref, core, slice(at + 2 * HEAD_DIM, at + 3 * HEAD_DIM))
+        slope = slope_ref[2 * pair + head]
+        for first in range(0, length, size):
+            side = core if first < half else 1 - core
+            rows_at = slice(first % half, first % half + size)
+            rows = qkv_ref[side, rows_at, at : at + HEAD_DIM] * jnp.bfloat16(HEAD_DIM**-0.5)
+            stop = first + size
+            parts = scores_of(
+                keys[:stop], rows, slope, seg_col, row_ref[:, first:stop], first, size
+            )
+            top = jnp.max(parts[-1], axis=0, keepdims=True)
+            if len(parts) > 1:
+                top = jnp.maximum(top, jnp.max(parts[0], axis=0, keepdims=True))
+            weights = [jnp.exp(part - top) for part in parts]
+            total = sum(jnp.sum(part, axis=0, keepdims=True) for part in weights)
+            log_total = top + jnp.log(total)
+            inverse = 1.0 / total
+            probs = [(part * inverse).astype(jnp.bfloat16) for part in weights]
+            if len(probs) > 1:
+                probs = jnp.concatenate(probs, axis=0)
+            else:
+                probs = probs[0]
+            out = tn(values[:stop], probs)
+            mixed_ref[side, rows_at, head * HEAD_DIM : (head + 1) * HEAD_DIM] = out.T.astype(
+                jnp.bfloat16
+            )
+            total_ref[0, head : head + 1, first:stop] = log_total
+
+
+def attend_back_kernel(
+    core_ref,
+    slope_ref,
+    qkv_ref,
+    grad_ref,
+    total_ref,
+    col_ref,
+    row_ref,
+    out_ref,
+    sums_ref,
+    probs_ref,
+    deltas_ref,
+):
+    pair = pl.program_id(0)
+    core = core_ref[0]
+    half = qkv_ref.shape[1]
+    length = 2 * half
+    size = min(PIECE, half)
+    scale = HEAD_DIM**-0.5
+    seg_col = col_ref[...]
+    sums = []
+    for head in range(2):
+        at = head * 3 * HEAD_DIM
+        keys = both_halves(qkv_ref, core, slice(at + HEAD_DIM, at + 2 * HEAD_DIM))
+        values = both_halves(qkv_ref, core, slice(at + 2 * HEAD_DIM, at + 3 * HEAD_DIM))
+        query = both_halves(qkv_ref, core, slice(at, at + HEAD_DIM)) * jnp.bfloat16(scale)
+        grads = both_halves(grad_ref, core, slice(head * HEAD_DIM, (head + 1) * HEAD_DIM))
+        slope = slope_ref[2 * pair + head]
+        query_sum = jnp.zeros((1, HEAD_DIM), jnp.float32)
+        value_sum = jnp.zeros((1, HEAD_DIM), jnp.float32)
+        for first in range(0, length, size):
+            side = core if first < half else 1 - core
+            rows_at = slice(first % half, first % half + size)
+            stop = first + size
+            parts = scores_of(
+                keys[:stop], query[first:stop], slope, seg_col, row_ref[:, first:stop], first, size
+            )
+            log_total = total_ref[0, head : head + 1, first:stop]
+            grad_probs = nt(values[:stop], grads[first:stop])
+            probs = [jnp.exp(part - log_total) for part in parts]
+            if len(probs) > 1:
+                probs = jnp.concatenate(probs, axis=0)
+            else:
+                probs = probs[0]
+            flow = probs * grad_probs
+            inner = jnp.sum(flow, axis=0, keepdims=True)
+            deltas = (flow - probs * inner).astype(jnp.bfloat16)
+            probs_ref[:stop, first:stop] = probs.astype(jnp.bfloat16)
+            deltas_ref[:stop, first:stop] = deltas
+            grad_query = (tn(keys[:stop], deltas).T * scale).astype(jnp.bfloat16)
+            query_sum = query_sum + jnp.sum(
+                grad_query.astype(jnp.float32), axis=0, keepdims=True
+            )
+            out_ref[side, rows_at, at : at + HEAD_DIM] = grad_query
+        for first in range(0, length, size):
+            side = core if first < half else 1 - core
+            rows_at = slice(first % half, first % half + size)
+            stop = first + size
+            grad_keys = nn(deltas_ref[first:stop, first:], query[first:]).astype(jnp.bfloat16)
+            grad_values = nn(probs_ref[first:stop, first:], grads[first:]).astype(jnp.bfloat16)
+            value_sum = value_sum + jnp.sum(
+                grad_values.astype(jnp.float32), axis=0, keepdims=True
+            )
+            out_ref[side, rows_at, at + HEAD_DIM : at + 2 * HEAD_DIM] = grad_keys
+            out_ref[side, rows_at, at + 2 * HEAD_DIM : at + 3 * HEAD_DIM] = grad_values
+        sums += [query_sum, value_sum]
+    sums_ref[0] = jnp.concatenate(sums, axis=1)
+
+
+def attend(core, slopes, qkv, seg_col, seg_row):
+    half = qkv.shape[1]
+    heads = qkv.shape[2] // (3 * HEAD_DIM)
+    pairs = heads // 2
+    length = 2 * half
+    flops = 4 * heads * length * length * HEAD_DIM
+    return pl.pallas_call(
+        attend_kernel,
+        grid_spec=pltpu.PrefetchScalarGridSpec(
+            num_scalar_prefetch=2,
+            grid=(pairs,),
+            in_specs=[
+                pl.BlockSpec((2, half, 6 * HEAD_DIM), lambda p, c, s: (0, 0, p)),
+                pl.BlockSpec((length, 1), lambda p, c, s: (0, 0)),
+                pl.BlockSpec((1, length), lambda p, c, s: (0, 0)),
+            ],
+            out_specs=[
+                pl.BlockSpec((2, half, 2 * HEAD_DIM), lambda p, c, s: (0, 0, p)),
+                pl.BlockSpec((1, 2, length), lambda p, c, s: (p, 0, 0)),
+            ],
+        ),
+        out_shape=[
+            jax.ShapeDtypeStruct((2, half, heads * HEAD_DIM), jnp.bfloat16),
+            jax.ShapeDtypeStruct((pairs, 2, length), jnp.float32),
+        ],
+        compiler_params=pltpu.CompilerParams(vmem_limit_bytes=48 * 2**20),
+        cost_estimate=pl.CostEstimate(
+            flops=4 * flops, bytes_accessed=6 * 2**20, transcendentals=heads * length * length
+        ),
+        name="attend_forward",
+    )(core, slopes, qkv, seg_col, seg_row)
+
+
+def attend_back(core, slopes, qkv, grads, totals, seg_col, seg_row):
+    half = qkv.shape[1]
+    heads = qkv.shape[2] // (3 * HEAD_DIM)
+    pairs = heads // 2
+    length = 2 * half
+    flops = 10 * heads * length * length * HEAD_DIM
+    return pl.pallas_call(
+        attend_back_kernel,
+        grid_spec=pltpu.PrefetchScalarGridSpec(
+            num_scalar_prefetch=2,
+            grid=(pairs,),
+            in_specs=[
+                pl.BlockSpec((2, half, 6 * HEAD_DIM), lambda p, c, s: (0, 0, p)),
+                pl.BlockSpec((2, half, 2 * HEAD_DIM), lambda p, c, s: (0, 0, p)),
+                pl.BlockSpec((1, 2, length), lambda p, c, s: (p, 0, 0)),
+                pl.BlockSpec((length, 1), lambda p, c, s: (0, 0)),
+                pl.BlockSpec((1, length), lambda p, c, s: (0, 0)),
+            ],
+            out_specs=[
+                pl.BlockSpec((2, half, 6 * HEAD_DIM), lambda p, c, s: (0, 0, p)),
+                pl.BlockSpec((1, 1, 4 * HEAD_DIM), lambda p, c, s: (p, 0, 0)),
+            ],
+            scratch_shapes=[
+                pltpu.VMEM((length, length), jnp.bfloat16),
+                pltpu.VMEM((length, length), jnp.bfloat16),
+            ],
+        ),
+        out_shape=[
+            jax.ShapeDtypeStruct(qkv.shape, jnp.bfloat16),
+            jax.ShapeDtypeStruct((pairs, 1, 4 * HEAD_DIM), jnp.float32),
+        ],
+        compiler_params=pltpu.CompilerParams(vmem_limit_bytes=48 * 2**20),
+        cost_estimate=pl.CostEstimate(
+            flops=4 * flops, bytes_accessed=10 * 2**20, transcendentals=heads * length * length
+        ),
+        name="attend_backward",
+    )(core, slopes, qkv, grads, totals, seg_col, seg_row)
+
+
+def join_kernel(code_ref, far_ref, own_ref, *rest):
+    parts, out_ref, sems = rest[:-2], rest[-2], rest[-1]
+    count = len(parts)
+    rows = out_ref.shape[0] // count
+    for piece in range(count):
+        spot = pl.ds(piece * rows, rows)
+
+        @pl.when(far_ref[0] == 0)
+        def _():
+            pltpu.make_async_copy(own_ref.at[spot], out_ref.at[spot], sems.at[piece]).start()
+
+        for slot in range(count):
+
+            @pl.when((far_ref[0] != 0) & (jnp.bitwise_xor(code_ref[0], slot) == piece))
+            def _():
+                pltpu.make_async_copy(parts[slot], out_ref.at[spot], sems.at[piece]).start()
+
+    for piece in range(count):
+        spot = pl.ds(piece * rows, rows)
+        pltpu.make_async_copy(own_ref.at[spot], out_ref.at[spot], sems.at[piece]).wait()
+
+
+def join(code, far, own, parts):
+    hbm = pl.BlockSpec(memory_space=pl.ANY)
+    smem = pl.BlockSpec(memory_space=pltpu.SMEM)
+    return pl.pallas_call(
+        join_kernel,
+        in_specs=[smem, smem, hbm] + [hbm] * len(parts),
+        out_specs=hbm,
+        out_shape=jax.ShapeDtypeStruct(own.shape, own.dtype),
+        scratch_shapes=[pltpu.SemaphoreType.DMA((len(parts),))],
+        cost_estimate=pl.CostEstimate(
+            flops=0, bytes_accessed=4 * own.size, transcendentals=0
+        ),
+        name="join_pieces",
+    )(code, far, own, *parts)
+
+
+def norm_parts(values):
+    row_mean = jnp.mean(values, axis=-1, keepdims=True)
+    centered = values - row_mean
+    row_var = jnp.mean(centered * centered, axis=-1, keepdims=True)
+    inverse = lax.rsqrt(row_var + norm_eps)
+    return centered * inverse, inverse
+
+
+def norm_back(values, gain, grads):
+    hat, inverse = norm_parts(values)
+    scaled = grads * gain
+    out = inverse * (
+        scaled
+        - jnp.mean(scaled, axis=-1, keepdims=True)
+        - hat * jnp.mean(scaled * hat, axis=-1, keepdims=True)
+    )
+    return out, jnp.sum(grads * hat, axis=0), jnp.sum(grads, axis=0)
+
+
+def halve(kept, came, bit, index):
+    outer = kept.shape[0] // (2 * bit)
+
+    def pick(value, which):
+        value = value.reshape((outer, 2, bit) + value.shape[1:])
+        return lax.dynamic_index_in_dim(value, which, 1, keepdims=False).reshape(
+            (outer * bit,) + value.shape[3:]
+        )
+
+    def part(which):
+        value = pick(kept, which).astype(jnp.float32)
+        if came is not None:
+            value = value + pick(came, which).astype(jnp.float32)
+        return value.astype(jnp.bfloat16)
+
+    return part(index), part(1 - index)
+
+
+def reduce_rows(grads, order, places):
+    core, y_at, z_low, z_high = places
+    width = grads.shape[1]
+    kept = grads.reshape(16, grads.shape[0] // 16, width)
+    came = None
+    left = ["core", "y", "low", "high"]
+    spot = {"core": core, "y": y_at, "low": z_low, "high": z_high}
+    flips = {"core": 1, "y": 2, "low": 4, "high": 8}
+    for step in order:
+        if step == "x":
+            total = kept if came is None else (
+                kept.astype(jnp.float32) + came.astype(jnp.float32)
+            ).astype(jnp.bfloat16)
+            kept, came = swap(total), None
+            continue
+        bit = 1 << left.index(step)
+        mine, other = halve(kept, came, bit, spot[step])
+        kept, came = mine, flip(other, flips[step])
+        left.remove(step)
+    return (kept.astype(jnp.float32) + came.astype(jnp.float32))[0]
+
+
+def sum_everywhere(value):
+    value = value + lax.ppermute(value, "tensor", [(0, 1), (1, 0)])
+    for bit in (1, 2, 4, 8):
+        value = value + flip(value, bit)
+    return value
+
+
+def chip_body(
+    tokens,
+    segments,
+    w_qkv,
+    b_qv,
+    w_out,
+    b_out,
+    w_up,
+    b_up,
+    w_down,
+    b_down,
+    gain_one,
+    shift_one,
+    gain_two,
+    shift_two,
+    cotangent,
+):
+    f32, bf16 = jnp.float32, jnp.bfloat16
+    place = lax.axis_index("dp")
+    rank = lax.axis_index("tensor")
+    core = core_of(place)
+    y_at = (place // 2) % 2
+    z_low = (place // 4) % 2
+    z_high = place // 8
+    places = (core, y_at, z_low, z_high)
+    far = (core != rank).astype(jnp.int32).reshape(1)
+    core_s = core.astype(jnp.int32).reshape(1)
+    half, width = tokens.shape
+    length = segments.shape[1]
+    heads = w_qkv.shape[1] // (3 * HEAD_DIM)
+
+    def fetch(weight, ways, gate):
+        rows = weight.shape[0] // ways
+        code = y_at if ways == 2 else z_low * 2 + y_at
+        piece = lax.dynamic_slice_in_dim(weight, code * rows, rows, 0)
+        piece = after(piece, gate) if gate is not None else piece
+        first = swap_far(piece)
+        parts = [first, flip_far(first, 2)]
+        if ways == 4:
+            parts += [flip_far(parts[0], 4), flip_far(parts[1], 4)]
+        return join(code.astype(jnp.int32).reshape(1), far, weight, parts), first
+
+    source_b = swap(tokens)
+    qkv_w, gate = fetch(w_qkv, 2, source_b)
+    b_qv_l = swap(b_qv)
+    b_up_l = swap(b_up)
+    out_w, gate = fetch(w_out, 2, gate)
+    up_w, gate = fetch(w_up, 4, gate)
+    seed_mine = swap(after(cotangent, gate))
+    down_w, gate = fetch(w_down, 4, seed_mine)
+    segment = jnp.where(core == rank, segments, flip(segments, 1))
+    seg_col = segment.reshape(length, 1)
+
+    head_index = core * heads + lax.iota(jnp.int32, heads)
+    slopes = 2.0 ** (-8.0 * (head_index + 1).astype(f32) / HEADS)
+    gain_one_f = gain_one.astype(f32)
+    gain_two_f = gain_two.astype(f32)
+
+    source = source_b.astype(f32)
+    normed = layer_norm(source, gain_one_f, shift_one.astype(f32)).astype(bf16)
+    rows_one = jnp.concatenate([normed, flip(normed, 1)], axis=0)
+    pair = b_qv_l.astype(f32).reshape(heads, 2, HEAD_DIM)
+    bias = jnp.stack([pair[:, 0], jnp.zeros_like(pair[:, 0]), pair[:, 1]], axis=1).reshape(-1)
+    joined = (jnp.dot(rows_one, qkv_w, preferred_element_type=f32) + bias).astype(bf16)
+    joined = joined.reshape(2, half, joined.shape[1])
+    mixed, totals = attend(core_s, slopes, joined, seg_col, segment)
+
+    came = flip(jnp.dot(mixed[1], out_w, preferred_element_type=f32).astype(bf16), 1)
+    resid = (
+        source
+        + jnp.dot(mixed[0], out_w, preferred_element_type=f32)
+        + came.astype(f32)
+        + b_out.astype(f32)
+    )
+    normed = layer_norm(resid, gain_two_f, shift_two.astype(f32)).astype(bf16)
+    rows_two = jnp.concatenate([normed, flip(normed, 1)], axis=0)
+    seed_rows = jnp.concatenate([seed_mine, flip(seed_mine, 1)], axis=0)
+    pre_act = jnp.dot(rows_two, up_w, preferred_element_type=f32) + b_up_l.astype(f32)
+    hidden, gelu_pull = jax.vjp(partial(jax.nn.gelu, approximate=True), pre_act)
+    slope_act = gelu_pull(jnp.ones_like(pre_act))[0].astype(bf16)
+    hidden = hidden.astype(bf16)
+    came = flip(jnp.dot(hidden[half:], down_w, preferred_element_type=f32).astype(bf16), 1)
+    layer_out = (
+        resid
+        + jnp.dot(hidden[:half], down_w, preferred_element_type=f32)
+        + came.astype(f32)
+        + b_down.astype(f32)
+    )
+    layer_out = swap(layer_out.astype(bf16))
+
+    grad_pre_f = contract_cols(seed_rows, down_w) * slope_act.astype(f32)
+    grad_pre = grad_pre_f.astype(bf16)
+    grad_b_up = jnp.sum(grad_pre.astype(f32), axis=0)
+    came = flip(contract_cols(grad_pre[half:], up_w).astype(bf16), 1)
+    grad_normed = contract_cols(grad_pre[:half], up_w) + came.astype(f32)
+    grad_down = contract_rows(seed_rows, hidden).astype(bf16)
+    sum_down = reduce_rows(grad_down, ("x", "core", "y", "low", "high"), places).T
+    grad_up = contract_rows(rows_two, grad_pre).astype(bf16)
+    sum_up = reduce_rows(grad_up, ("y", "x", "core", "low", "high"), places)
+    grad_norm, grad_gain_two, grad_shift_two = norm_back(resid, gain_two_f, grad_normed)
+    seed = seed_mine.astype(f32)
+    grad_resid = seed + grad_norm
+    branch = grad_resid.astype(bf16)
+    branch_rows = jnp.concatenate([branch, flip(branch, 1)], axis=0)
+    grad_mixed = contract_cols(branch_rows, out_w).astype(bf16).reshape(mixed.shape)
+    grad_joined, qv_sums = attend_back(core_s, slopes, joined, grad_mixed, totals, seg_col, segment)
+    grad_out = contract_rows(branch_rows, mixed.reshape(2 * half, -1)).astype(bf16)
+    sum_out = reduce_rows(grad_out, ("x", "core", "y", "low", "high"), places).T
+    grad_joined = grad_joined.reshape(2 * half, -1)
+    grad_qkv = contract_rows(rows_one, grad_joined).astype(bf16)
+    sum_qkv = reduce_rows(grad_qkv, ("y", "x", "core", "low", "high"), places)
+    came = flip(contract_cols(grad_joined[half:], qkv_w).astype(bf16), 1)
+    grad_normed = contract_cols(grad_joined[:half], qkv_w) + came.astype(f32)
+    grad_source, grad_gain_one, grad_shift_one = norm_back(source, gain_one_f, grad_normed)
+    input_grad = swap((grad_resid + grad_source).astype(bf16))
+
+    early = sum_everywhere(
+        jnp.concatenate(
+            [
+                jnp.sum(grad_resid, axis=0),
+                grad_gain_two,
+                grad_shift_two,
+                jnp.sum(seed, axis=0),
+                spread_slots(grad_b_up, core, 2),
+            ]
+        )
+    )
+    late = sum_everywhere(
+        jnp.concatenate(
+            [grad_gain_one, grad_shift_one, spread_slots(qv_sums.reshape(-1), core, 2)]
+        )
+    )
+    up_width = grad_b_up.shape[0]
+    qv_width = b_qv.shape[0]
+    sum_b_up = lax.dynamic_slice_in_dim(early[4 * width :], rank * up_width, up_width)
+    sum_b_qv = lax.dynamic_slice_in_dim(late[2 * width :], rank * qv_width, qv_width)
+    return (
+        layer_out,
+        input_grad,
+        sum_qkv,
+        sum_b_qv,
+        sum_out,
+        early[:width],
+        sum_up,
+        sum_b_up,
+        sum_down,
+        early[3 * width : 4 * width],
+        late[:width],
+        late[width : 2 * width],
+        early[width : 2 * width],
+        early[2 * width : 3 * width],
+    )
+
+
 def solution(mesh):
     in_specs = (
         P(("dp", "tensor"), None),
@@ -310,4 +828,6 @@
         P(),
         P(),
     )
-    return jax.shard_map(body, mesh=mesh, in_specs=in_specs, out_specs=out_specs, check_vma=False)
+    pairs = mesh.shape["tensor"] == 2 and mesh.shape["dp"] == 16
+    plan = chip_body if pairs else body
+    return jax.shard_map(plan, mesh=mesh, in_specs=in_specs, out_specs=out_specs, check_vma=False)

time: 673 us -> 807 us (1.20)
  Pallas kernels: 0 us -> 430 us
  waiting for transfers between devices: 322 us -> 107 us
  starting transfers between devices: 0.67 us -> 145 us
  matrix products: 179 us -> 76.6 us
  other arithmetic: 84 us -> 17.3 us
  blocking collectives: 41.7 us -> 0 us
  between operations: 15.1 us -> 2.21 us
    pallas_call x0 -> x6, Pallas kernels: none -> 430 us  [the longest x4 386 us: join(): pl.pallas_call(join_kernel, in_specs=[smem, smem, hbm] + [hbm] * len(part...]
    reduce_scatter x8 -> x0, waiting for transfers between devices: 222 us -> none  [the longest x1 58.6 us: body(): lax.psum_scatter(grad_out.astype(jnp.bfloat16), 'dp', scatter_dimension=1...]
    ppermute x0 -> x57, starting transfers between devices: none -> 145 us  [the longest x33 90 us: flip(): return lax.ppermute(value, 'dp', flip_pairs(bit))]
    ppermute x0 -> x57, waiting for transfers between devices: none -> 107 us  [the longest x33 76.8 us: flip(): return lax.ppermute(value, 'dp', flip_pairs(bit))]
    all_gather x4 -> x0, waiting for transfers between devices: 99.6 us -> none  [the longest x1 32.6 us: body(): rows_two = lax.all_gather(normed_two, 'tensor', axis=0, tiled=True)]
    dot_general x16 -> x6, matrix products: 121 us -> 27.8 us  [the longest x1 13.3 us: chip_body(): jnp.dot(rows_two, up_w, preferred_element_type=f32) + b_up_l.astype(f32)]
    psum x1 -> x0, blocking collectives: 41.7 us -> none  [body(): lax.psum((grad_gain_one, grad_shift_one, jnp.sum(grad_resid, axis=0), gra...]
    convert_element_type x22 -> x25, other arithmetic: 50.2 us -> 8.86 us  [the longest x2 3.05 us: reduce_rows(): total = kept if came is None else (kept.astype(jnp.float32) + came.astype...]
  transfers between devices with their start and end apart: 12 -> 57, of which waited for: 11 -> 13; matrix products, arithmetic and copies ran while one was open for 27% -> 11% of each run, Pallas kernels for 0% -> 38%
where the time goes in v1:
time: 807 us; the launch traced here: 797 us
  Pallas kernels  430 us (53%)
  starting transfers between devices  145 us (18%)
  waiting for transfers between devices  107 us (13%)
  matrix products  76.6 us (9%)
  local copies, waits for them, and re-layouts  19.5 us (2%)
  other arithmetic  17.3 us (2%)
    pallas_call x4, Pallas kernels, join(): pl.pallas_call(join_kernel, in_specs=[smem, smem, hbm] + [hbm] * len(part...  386 us
    ppermute x33, starting transfers between devices, flip(): return lax.ppermute(value, 'dp', flip_pairs(bit))  90 us
    ppermute x33, waiting for transfers between devices, flip(): return lax.ppermute(value, 'dp', flip_pairs(bit))  76.8 us
    ppermute x2, waiting for transfers between devices, sum_everywhere(): value = value + lax.ppermute(value, 'tensor', [(0, 1), (1, 0)])  29.8 us
    ppermute x10, starting transfers between devices, swap(): return lax.ppermute(value, ('dp', 'tensor'), swap_pairs())  28.4 us
    dot_general x6, matrix products, contract_cols(): lax.dot_general(left, right, (((1,), (1,)), ((), ())), preferred_element_...  26.2 us
    pallas_call x1, Pallas kernels, attend_back(): pl.pallas_call(attend_back_kernel, grid_spec=pltpu.PrefetchScalarGridSpec...  25.2 us
    dot_general x4, matrix products, contract_rows(): lax.dot_general(left, right, (((0,), (0,)), ((), ())), preferred_element_...  22.6 us
  transfers between devices with their start and end apart: 57, of which 13 were waited for; matrix products, arithmetic and copies ran while one was open for 11% of the time, Pallas kernels for 38%

profile of v1, /device:TPU:0, one launch (start us, length us, event | category | flops | bytes accessed | tf_op | source)
XLA Modules:
  0.0 797.2 jit_solution(2367137557922955267)
XLA Ops:
  2.7 2.6 constant_dynamic-slice_fusion.11
  14.8 41.2 %collective-permute-start.1 = (bf16[512,1024]{1,0:T(8,128)(2,1)}, bf16[512,1024]{1,0:T(8,128)(2,1)}, u32[]{:S(2)}, u32[]{:S(2)}) collective-permute-start(bf16[512,1024]{1,0:T(8,128)(2,1)} %fusion.16), channel_id=1, source_target_pairs={{0,2},{2,0},{4,6},{6,4},{8,10},{10,8},{12,14},{14,12},{16,18},{18,... | collective-permute-start | bytes 3145736 | tf_op jit(solution)/shard_map/ppermute | solution.py:313
  60.1 32.9 %join_pieces.5 = bf16[512,1024]{1,0:T(8,128)(2,1)} custom-call(s32[1]{0:T(128)} %bitcast.1.code_ref, s32[1]{0:T(128)} %bitcast.2.far_ref, bf16[512,1024]{1,0:T(8,128)(2,1)} %own_ref.5, bf16[256,1024]{1,0:T(8,128)(2,1)} %copy-done.13, bf16[256,1024]{1,0:T(8,128)(2,1)} %collective-permute-done.7.rest_1_), custom_call_target="tpu_custom_call" | custom-call | bytes 2097152 | tf_op jit(solution)/shard_map/join_pieces/pallas_call | solution.py:564
  93.0 9.5 %collective-permute-start.15 = (bf16[512,1024]{1,0:T(8,128)(2,1)}, bf16[512,1024]{1,0:T(8,128)(2,1)}, u32[]{:S(2)}, u32[]{:S(2)}) collective-permute-start(bf16[512,1024]{1,0:T(8,128)(2,1)} %param.29), channel_id=1, source_target_pairs={{0,0},{1,2},{2,1},{3,3},{4,4},{5,6},{6,5},{7,7},{8,8},{9,10},{10,9... | collective-permute-start | bytes 3145736 | tf_op jit(solution)/shard_map/ppermute | solution.py:305
  102.5 96.4 %join_pieces.4 = bf16[1024,1536]{1,0:T(8,128)(2,1)} custom-call(s32[1]{0:T(128)} %bitcast.1.code_ref, s32[1]{0:T(128)} %bitcast.2.far_ref, bf16[1024,1536]{1,0:T(8,128)(2,1)} %own_ref.4, bf16[512,1536]{1,0:T(8,128)(2,1)} %collective-permute-done.2.rest_0_, bf16[512,1536]{1,0:T(8,128)(2,1)} %collective-permute-done.3.rest_1_), custom_call_target="tpu_custom_call" | custom-call | bytes 6291456 | tf_op jit(solution)/shard_map/join_pieces/pallas_call | solution.py:564
  199.0 5.9 add_convert_fusion
  204.9 18.9 %attend_forward.1 = (bf16[2,512,512]{2,1,0:T(8,128)(2,1)S(1)}, f32[4,2,1024]{2,1,0:T(2,128)S(1)}) custom-call(s32[1]{0:T(128)} %bitcast.core_ref, f32[8]{0:T(128)S(1)} %multiply_power_fusion.slope_ref, bf16[2,512,1536]{2,1,0:T(8,128)(2,1)S(1)} %bitcast.159, s32[1024,1]{1,0:T(8,128)S(1)} %copy.39.col_ref, s32[1,1024]{1,0:T(1,128)S(1)} %broadcast_select_fusion.row_ref), custom_call_target="tpu_custom_call" | custom-call | flops 8589934592 | bytes 6291456 | tf_op jit(solution)/shard_map/attend_forward/pallas_call | solution.py:473
  225.6 12.5 %collective-permute-start.8 = (bf16[512,1024]{1,0:T(8,128)(2,1)}, bf16[512,1024]{1,0:T(8,128)(2,1)}, u32[]{:S(2)}, u32[]{:S(2)}) collective-permute-start(bf16[512,1024]{1,0:T(8,128)(2,1)} %convolution_convert_fusion.5), channel_id=1, source_target_pairs={{0,2},{2,0},{4,6},{6,4},{8,10},{10,8},{12,14},{14,12},{16,18},{18,... | collective-permute-start | bytes 3145736 | tf_op jit(solution)/shard_map/ppermute | solution.py:313
  245.3 6.6 collective-permute-start.22
  253.6 2.2 fusion.83
  259.2 7.4 collective-permute-start.9
  266.6 2.3 constant_dynamic-update-slice_fusion.1
  270.7 128.2 %join_pieces.6 = bf16[1024,2048]{1,0:T(8,128)(2,1)} custom-call(s32[1]{0:T(128)} %bitcast.7.code_ref, s32[1]{0:T(128)} %bitcast.2.far_ref, bf16[1024,2048]{1,0:T(8,128)(2,1)} %own_ref.6, bf16[256,2048]{1,0:T(8,128)(2,1)} %collective-permute-done.10.rest_0_, bf16[256,2048]{1,0:T(8,128)(2,1)} %collective-permute-done.11.rest_1_, ...), custom_call_target="tpu_custom_call" | custom-call | bytes 8388608 | tf_op jit(solution)/shard_map/join_pieces/pallas_call | solution.py:564
  398.9 2.3 constant_dynamic-update-slice_fusion
  402.9 13.3 %multiply_convert_fusion.1 = (bf16[1024,2048]{1,0:T(8,128)(2,1)}, f32[1024,2048]{1,0:T(8,128)}) fusion(f32[2048]{0:T(1024)S(1)} %convert_element_type.550, bf16[1024,2048]{1,0:T(8,128)(2,1)} %join_pieces.6, bf16[512,1024]{1,0:T(8,128)(2,1)} %collective-permute-done.9, bf16[512,1024]{1,0:T(8,128)(2,1)} %add_convert_fusion.4), kind=kOutput, calls=%fused_computation.11 | convolution fusion | flops 4320133120 | bytes 18882560 | tf_op jit(solution)/shard_map/dot_general | solution.py:720
  416.1 128.2 %join_pieces.7 = bf16[2048,1024]{1,0:T(8,128)(2,1)} custom-call(s32[1]{0:T(128)} %bitcast.7.code_ref, s32[1]{0:T(128)} %bitcast.2.far_ref, bf16[2048,1024]{1,0:T(8,128)(2,1)} %own_ref.7, bf16[512,1024]{1,0:T(8,128)(2,1)} %collective-permute-done.16.rest_0_, bf16[512,1024]{1,0:T(8,128)(2,1)} %collective-permute-done.17.rest_1_, ...), custom_call_target="tpu_custom_call" | custom-call | bytes 8388608 | tf_op jit(solution)/shard_map/join_pieces/pallas_call | solution.py:564
  544.4 13.3 %convert_reduce_fusion = (f32[2048]{0:T(1024)S(1)}, bf16[1024,2048]{1,0:T(8,128)(2,1)S(1)}) fusion(f32[1024,2048]{1,0:T(8,128)} %get-tuple-element.76, f32[2048]{0:T(1024)S(1)} %convert_element_type.550, bf16[1024,1024]{1,0:T(8,128)(2,1)} %constant_dynamic-update-slice_fusion, bf16[2048,1024]{1,0:T(8,128)(2,1)} %join_pieces.7), kind=kOutput, calls=%fused_computation.9 | convolution fusion | flops 4345296896 | bytes 18890752 | tf_op jit(solution)/shard_map/dot_general | solution.py:32
  557.8 2.4 fusion.50
  560.1 2.9 collective-permute-start.23
  563.1 2.3 fusion.47
  565.4 2.6 collective-permute-start.20
  568.0 2.3 fusion.32
  570.5 3.1 multiply_reduce_fusion
  573.5 3.9 fusion.79
  577.5 3.1 collective-permute-start.42
  580.6 2.1 collective-permute-done.42
  584.4 9.5 %convolution_convert_fusion.1 = bf16[1024,2048]{1,0:T(8,128)(2,1)} fusion(bf16[1024,1024]{1,0:T(8,128)(2,1)} %constant_dynamic-update-slice_fusion, bf16[1024,2048]{1,0:T(8,128)(2,1)} %get-tuple-element.75), kind=kOutput, calls=%fused_computation.16 | convolution fusion | flops 4297064448 | bytes 10485760 | tf_op jit(solution)/shard_map/dot_general | solution.py:26
  593.9 2.8 collective-permute-start.52
  599.7 6.4 convolution_convert_fusion.2
  606.2 2.7 collective-permute-start.46
  612.0 9.5 %collective-permute-start.21 = (bf16[512,1024]{1,0:T(8,128)(2,1)}, bf16[512,1024]{1,0:T(8,128)(2,1)}, u32[]{:S(2)}, u32[]{:S(2)}) collective-permute-start(bf16[512,1024]{1,0:T(8,128)(2,1)} %get-tuple-element.54), channel_id=1, source_target_pairs={{0,0},{1,2},{2,1},{3,3},{4,4},{5,6},{6,5},{7,7},{8,8},{9,10},{10,9... | collective-permute-start | bytes 3145736 | tf_op jit(solution)/shard_map/ppermute | solution.py:305
  624.1 25.2 %attend_backward.1 = (bf16[2,512,1536]{2,1,0:T(8,128)(2,1)S(1)}, f32[4,1,256]{2,1,0:T(1,128)S(1)}) custom-call(s32[1]{0:T(128)} %bitcast.core_ref, f32[8]{0:T(128)S(1)} %multiply_power_fusion.slope_ref, bf16[2,512,1536]{2,1,0:T(8,128)(2,1)} %bitcast.160, bf16[2,512,512]{2,1,0:T(8,128)(2,1)S(1)} %bitcast.163, f32[4,2,1024]{2,1,0:T(2,128)S(1)} %get-tuple-element.29.total_ref, ...), custom_call_target="tpu_custom_call" | custom-call | flops 21474836480 | bytes 10485760 | tf_op jit(solution)/shard_map/attend_backward/pallas_call | solution.py:506
  649.3 3.7 fusion.44
  653.1 5.4 convolution_convert_fusion
  662.1 2.5 fusion.7
  665.7 2.4 fusion.22
  668.1 4.5 collective-permute-start.32
  673.2 27.7 %collective-permute-done.32 = f32[4096]{0:T(1024)S(1)} collective-permute-done((f32[4096]{0:T(1024)S(1)}, f32[4096]{0:T(1024)S(1)}, u32[]{:S(2)}, u32[]{:S(2)}) %collective-permute-start.32) | collective-permute-done | bytes 16416 | tf_op jit(solution)/shard_map/ppermute | solution.py:637
  702.7 3.1 collective-permute-done.34
  706.5 3.1 collective-permute-done.35
  712.0 2.3 collective-permute-done.36
  719.0 5.5 collective-permute-done.39
  726.2 3.6 collective-permute-done.40
  731.9 15.0 %collective-permute-done.54 = bf16[4,64,2048]{2,1,0:T(8,128)(2,1)S(1)} collective-permute-done((bf16[4,64,2048]{2,1,0:T(8,128)(2,1)S(1)}, bf16[4,64,2048]{2,1,0:T(8,128)(2,1)S(1)}, u32[]{:S(2)}, u32[]{:S(2)}) %collective-permute-start.54) | collective-permute-done | bytes 1048608 | tf_op jit(solution)/shard_map/ppermute | solution.py:313
  748.4 18.0 %collective-permute-done.55 = bf16[2,64,2048]{2,1,0:T(8,128)(2,1)S(1)} collective-permute-done((bf16[2,64,2048]{2,1,0:T(8,128)(2,1)S(1)}, bf16[2,64,2048]{2,1,0:T(8,128)(2,1)S(1)}, u32[]{:S(2)}, u32[]{:S(2)}) %collective-permute-start.55) | collective-permute-done | bytes 524320 | tf_op jit(solution)/shard_map/ppermute | solution.py:313
  767.8 14.9 %collective-permute-done.30 = bf16[2,64,1536]{2,1,0:T(8,128)(2,1)S(1)} collective-permute-done((bf16[2,64,1536]{2,1,0:T(8,128)(2,1)S(1)}, bf16[2,64,1536]{2,1,0:T(8,128)(2,1)S(1)}, u32[]{:S(2)}, u32[]{:S(2)}) %collective-permute-start.30) | collective-permute-done | bytes 393248 | tf_op jit(solution)/shard_map/ppermute | solution.py:313
  783.8 8.9 %collective-permute-done.31 = bf16[1,64,1536]{2,1,0:T(8,128)(2,1)S(1)} collective-permute-done((bf16[1,64,1536]{2,1,0:T(8,128)(2,1)S(1)}, bf16[1,64,1536]{2,1,0:T(8,128)(2,1)S(1)}, u32[]{:S(2)}, u32[]{:S(2)}) %collective-permute-start.31) | collective-permute-done | bytes 196640 | tf_op jit(solution)/shard_map/ppermute | solution.py:313
  793.5 2.3 copy.64
  (233 shorter events, 67.5 us)
Async XLA Ops:
  0.7 4.7 collective-permute-start
  9.5 93.0 %collective-permute-start.3 = (bf16[512,1536]{1,0:T(8,128)(2,1)}, bf16[512,1536]{1,0:T(8,128)(2,1)}, u32[]{:S(2)}, u32[]{:S(2)}) collective-permute-start(bf16[512,1536]{1,0:T(8,128)(2,1)} %collective-permute-done.2.rest_0_), channel_id=1, source_target_pairs={{1,5},{2,6},{5,1},{6,2},{9,13},{10,14},{13,9},{14,10},{17,21},{18,... | collective-permute-start | bytes 4718600 | tf_op jit(solution)/shard_map/ppermute | solution.py:317
  11.8 81.3 %collective-permute-start.10 = (bf16[256,2048]{1,0:T(8,128)(2,1)S(1)}, bf16[256,2048]{1,0:T(8,128)(2,1)}, u32[]{:S(2)}, u32[]{:S(2)}) collective-permute-start(bf16[256,2048]{1,0:T(8,128)(2,1)S(1)} %constant_dynamic-slice_fusion.9), channel_id=1, source_target_pairs={{1,2},{2,1},{5,6},{6,5},{9,10},{10,9},{13,14},{14,13},{17,18},{18,... | collective-permute-start | bytes 3145736 | tf_op jit(solution)/shard_map/ppermute | solution.py:309
  14.8 184.1 %collective-permute-start.1 = (bf16[512,1024]{1,0:T(8,128)(2,1)}, bf16[512,1024]{1,0:T(8,128)(2,1)}, u32[]{:S(2)}, u32[]{:S(2)}) collective-permute-start(bf16[512,1024]{1,0:T(8,128)(2,1)} %fusion.16), channel_id=1, source_target_pairs={{0,2},{2,0},{4,6},{6,4},{8,10},{10,8},{12,14},{14,12},{16,18},{18,... | collective-permute-start | bytes 3145736 | tf_op jit(solution)/shard_map/ppermute | solution.py:313
  93.0 150.6 %collective-permute-start.15 = (bf16[512,1024]{1,0:T(8,128)(2,1)}, bf16[512,1024]{1,0:T(8,128)(2,1)}, u32[]{:S(2)}, u32[]{:S(2)}) collective-permute-start(bf16[512,1024]{1,0:T(8,128)(2,1)} %param.29), channel_id=1, source_target_pairs={{0,0},{1,2},{2,1},{3,3},{4,4},{5,6},{6,5},{7,7},{8,8},{9,10},{10,9... | collective-permute-start | bytes 3145736 | tf_op jit(solution)/shard_map/ppermute | solution.py:305
  225.6 19.7 %collective-permute-start.8 = (bf16[512,1024]{1,0:T(8,128)(2,1)}, bf16[512,1024]{1,0:T(8,128)(2,1)}, u32[]{:S(2)}, u32[]{:S(2)}) collective-permute-start(bf16[512,1024]{1,0:T(8,128)(2,1)} %convolution_convert_fusion.5), channel_id=1, source_target_pairs={{0,2},{2,0},{4,6},{6,4},{8,10},{10,8},{12,14},{14,12},{16,18},{18,... | collective-permute-start | bytes 3145736 | tf_op jit(solution)/shard_map/ppermute | solution.py:313
  238.1 13.8 %collective-permute-start.11 = (bf16[256,2048]{1,0:T(8,128)(2,1)}, bf16[256,2048]{1,0:T(8,128)(2,1)}, u32[]{:S(2)}, u32[]{:S(2)}) collective-permute-start(bf16[256,2048]{1,0:T(8,128)(2,1)} %collective-permute-done.10.rest_0_), channel_id=1, source_target_pairs={{1,5},{2,6},{5,1},{6,2},{9,13},{10,14},{13,9},{14,10},{17,21},{18,... | collective-permute-start | bytes 3145736 | tf_op jit(solution)/shard_map/ppermute | solution.py:317
  239.8 19.4 %collective-permute-start.14 = (bf16[2048]{0:T(1024)(128)(2,1)S(1)}, bf16[2048]{0:T(1024)(128)(2,1)S(1)}, u32[]{:S(2)}, u32[]{:S(2)}) collective-permute-start(bf16[2048]{0:T(1024)(128)(2,1)S(1)} %copy-done.23), channel_id=1, source_target_pairs={{0,0},{1,2},{2,1},{3,3},{4,4},{5,6},{6,5},{7,7},{8,8},{9,10},{10,9... | collective-permute-start | bytes 12296 | tf_op jit(solution)/shard_map/ppermute | solution.py:305
  241.9 27.0 %collective-permute-start.12 = (bf16[256,2048]{1,0:T(8,128)(2,1)}, bf16[256,2048]{1,0:T(8,128)(2,1)}, u32[]{:S(2)}, u32[]{:S(2)}) collective-permute-start(bf16[256,2048]{1,0:T(8,128)(2,1)} %collective-permute-done.10.rest_0_), channel_id=1, source_target_pairs={{1,9},{2,10},{5,13},{6,14},{9,1},{10,2},{13,5},{14,6},{17,25},{18,... | collective-permute-start | bytes 3145736 | tf_op jit(solution)/shard_map/ppermute | solution.py:317
  243.6 14.0 %collective-permute-start.16 = (bf16[512,1024]{1,0:T(8,128)(2,1)S(1)}, bf16[512,1024]{1,0:T(8,128)(2,1)}, u32[]{:S(2)}, u32[]{:S(2)}) collective-permute-start(bf16[512,1024]{1,0:T(8,128)(2,1)S(1)} %constant_dynamic-slice_fusion.8), channel_id=1, source_target_pairs={{1,2},{2,1},{5,6},{6,5},{9,10},{10,9},{13,14},{14,13},{17,18},{18,... | collective-permute-start | bytes 3145736 | tf_op jit(solution)/shard_map/ppermute | solution.py:309
  245.3 153.7 %collective-permute-start.22 = (bf16[512,1024]{1,0:T(8,128)(2,1)}, bf16[512,1024]{1,0:T(8,128)(2,1)}, u32[]{:S(2)}, u32[]{:S(2)}) collective-permute-start(bf16[512,1024]{1,0:T(8,128)(2,1)} %collective-permute-done.15), channel_id=1, source_target_pairs={{0,2},{2,0},{4,6},{6,4},{8,10},{10,8},{12,14},{14,12},{16,18},{18,... | collective-permute-start | bytes 3145736 | tf_op jit(solution)/shard_map/ppermute | solution.py:313
  251.9 18.8 %collective-permute-start.13 = (bf16[256,2048]{1,0:T(8,128)(2,1)}, bf16[256,2048]{1,0:T(8,128)(2,1)}, u32[]{:S(2)}, u32[]{:S(2)}) collective-permute-start(bf16[256,2048]{1,0:T(8,128)(2,1)} %collective-permute-done.11.rest_1_), channel_id=1, source_target_pairs={{1,9},{2,10},{5,13},{6,14},{9,1},{10,2},{13,5},{14,6},{17,25},{18,... | collective-permute-start | bytes 3145736 | tf_op jit(solution)/shard_map/ppermute | solution.py:317
  257.6 143.7 %collective-permute-start.17 = (bf16[512,1024]{1,0:T(8,128)(2,1)}, bf16[512,1024]{1,0:T(8,128)(2,1)}, u32[]{:S(2)}, u32[]{:S(2)}) collective-permute-start(bf16[512,1024]{1,0:T(8,128)(2,1)} %collective-permute-done.16.rest_0_), channel_id=1, source_target_pairs={{1,5},{2,6},{5,1},{6,2},{9,13},{10,14},{13,9},{14,10},{17,21},{18,... | collective-permute-start | bytes 3145736 | tf_op jit(solution)/shard_map/ppermute | solution.py:317
  259.2 143.7 %collective-permute-start.9 = (bf16[512,1024]{1,0:T(8,128)(2,1)}, bf16[512,1024]{1,0:T(8,128)(2,1)}, u32[]{:S(2)}, u32[]{:S(2)}) collective-permute-start(bf16[512,1024]{1,0:T(8,128)(2,1)} %add_convert_fusion.4), channel_id=1, source_target_pairs={{0,2},{2,0},{4,6},{6,4},{8,10},{10,8},{12,14},{14,12},{16,18},{18,... | collective-permute-start | bytes 3145736 | tf_op jit(solution)/shard_map/ppermute | solution.py:313
  268.9 147.2 %collective-permute-start.18 = (bf16[512,1024]{1,0:T(8,128)(2,1)}, bf16[512,1024]{1,0:T(8,128)(2,1)}, u32[]{:S(2)}, u32[]{:S(2)}) collective-permute-start(bf16[512,1024]{1,0:T(8,128)(2,1)} %collective-permute-done.16.rest_0_), channel_id=1, source_target_pairs={{1,9},{2,10},{5,13},{6,14},{9,1},{10,2},{13,5},{14,6},{17,25},{18,... | collective-permute-start | bytes 3145736 | tf_op jit(solution)/shard_map/ppermute | solution.py:317
  401.2 14.9 %collective-permute-start.19 = (bf16[512,1024]{1,0:T(8,128)(2,1)}, bf16[512,1024]{1,0:T(8,128)(2,1)}, u32[]{:S(2)}, u32[]{:S(2)}) collective-permute-start(bf16[512,1024]{1,0:T(8,128)(2,1)} %collective-permute-done.17.rest_1_), channel_id=1, source_target_pairs={{1,9},{2,10},{5,13},{6,14},{9,1},{10,2},{13,5},{14,6},{17,25},{18,... | collective-permute-start | bytes 3145736 | tf_op jit(solution)/shard_map/ppermute | solution.py:317
  560.1 10.3 %collective-permute-start.23 = (bf16[512,1024]{1,0:T(8,128)(2,1)S(1)}, bf16[512,1024]{1,0:T(8,128)(2,1)S(1)}, u32[]{:S(2)}, u32[]{:S(2)}) collective-permute-start(bf16[512,1024]{1,0:T(8,128)(2,1)S(1)} %fusion.50), channel_id=1, source_target_pairs={{0,2},{2,0},{4,6},{6,4},{8,10},{10,8},{12,14},{14,12},{16,18},{18,... | collective-permute-start | bytes 3145736 | tf_op jit(solution)/shard_map/ppermute | solution.py:313
  565.4 8.1 %collective-permute-start.20 = (bf16[512,1024]{1,0:T(8,128)(2,1)S(1)}, bf16[512,1024]{1,0:T(8,128)(2,1)S(1)}, u32[]{:S(2)}, u32[]{:S(2)}) collective-permute-start(bf16[512,1024]{1,0:T(8,128)(2,1)S(1)} %fusion.47), channel_id=1, source_target_pairs={{0,2},{2,0},{4,6},{6,4},{8,10},{10,8},{12,14},{14,12},{16,18},{18,... | collective-permute-start | bytes 3145736 | tf_op jit(solution)/shard_map/ppermute | solution.py:313
  577.5 5.1 collective-permute-start.42
  583.8 14.2 %collective-permute-start.44 = (f32[8192]{0:T(1024)S(1)}, f32[8192]{0:T(1024)S(1)}, u32[]{:S(2)}, u32[]{:S(2)}) collective-permute-start(f32[8192]{0:T(1024)S(1)} %add.442), channel_id=1, source_target_pairs={{0,4},{2,6},{4,0},{6,2},{8,12},{10,14},{12,8},{14,10},{16,20},{18,... | collective-permute-start | bytes 98312 | tf_op jit(solution)/shard_map/ppermute | solution.py:313
  593.9 78.6 %collective-permute-start.52 = (bf16[16,64,2048]{2,1,0:T(8,128)(2,1)}, bf16[16,64,2048]{2,1,0:T(8,128)(2,1)S(1)}, u32[]{:S(2)}, u32[]{:S(2)}) collective-permute-start(bf16[16,64,2048]{2,1,0:T(8,128)(2,1)} %bitcast.51), channel_id=1, source_target_pairs={{0,0},{1,2},{2,1},{3,3},{4,4},{5,6},{6,5},{7,7},{8,8},{9,10},{10,9... | collective-permute-start | bytes 12582920 | tf_op jit(solution)/shard_map/ppermute | solution.py:305
  597.0 25.8 %collective-permute-start.24 = (bf16[512,1024]{1,0:T(8,128)(2,1)S(1)}, bf16[512,1024]{1,0:T(8,128)(2,1)S(1)}, u32[]{:S(2)}, u32[]{:S(2)}) collective-permute-start(bf16[512,1024]{1,0:T(8,128)(2,1)S(1)} %convert_element_type.562), channel_id=1, source_target_pairs={{0,2},{2,0},{4,6},{6,4},{8,10},{10,8},{12,14},{14,12},{16,18},{18,... | collective-permute-start | bytes 3145736 | tf_op jit(solution)/shard_map/ppermute | solution.py:313
  598.1 8.1 %collective-permute-start.45 = (f32[8192]{0:T(1024)S(1)}, f32[8192]{0:T(1024)S(1)}, u32[]{:S(2)}, u32[]{:S(2)}) collective-permute-start(f32[8192]{0:T(1024)S(1)} %add.443), channel_id=1, source_target_pairs={{0,8},{2,10},{4,12},{6,14},{8,0},{10,2},{12,4},{14,6},{16,24},{18,... | collective-permute-start | bytes 98312 | tf_op jit(solution)/shard_map/ppermute | solution.py:313
  606.2 15.4 %collective-permute-start.46 = (f32[8192]{0:T(1024)S(1)}, f32[8192]{0:T(1024)S(1)}, u32[]{:S(2)}, u32[]{:S(2)}) collective-permute-start(f32[8192]{0:T(1024)S(1)} %add.444), channel_id=1, source_target_pairs={{0,16},{2,18},{4,20},{6,22},{8,24},{10,26},{12,28},{14,30},{16,0},... | collective-permute-start | bytes 98312 | tf_op jit(solution)/shard_map/ppermute | solution.py:313
  610.5 51.6 %collective-permute-start.47 = (bf16[8,64,2048]{2,1,0:T(8,128)(2,1)}, bf16[8,64,2048]{2,1,0:T(8,128)(2,1)}, u32[]{:S(2)}, u32[]{:S(2)}) collective-permute-start(bf16[8,64,2048]{2,1,0:T(8,128)(2,1)} %bitcast.42), channel_id=1, source_target_pairs={{0,4},{2,6},{4,0},{6,2},{8,12},{10,14},{12,8},{14,10},{16,20},{18,... | collective-permute-start | bytes 6291464 | tf_op jit(solution)/shard_map/ppermute | solution.py:313
  612.0 49.3 %collective-permute-start.21 = (bf16[512,1024]{1,0:T(8,128)(2,1)}, bf16[512,1024]{1,0:T(8,128)(2,1)}, u32[]{:S(2)}, u32[]{:S(2)}) collective-permute-start(bf16[512,1024]{1,0:T(8,128)(2,1)} %get-tuple-element.54), channel_id=1, source_target_pairs={{0,0},{1,2},{2,1},{3,3},{4,4},{5,6},{6,5},{7,7},{8,8},{9,10},{10,9... | collective-permute-start | bytes 3145736 | tf_op jit(solution)/shard_map/ppermute | solution.py:305
  653.1 12.6 %collective-permute-start.25 = (bf16[512,1024]{1,0:T(8,128)(2,1)S(1)}, bf16[512,1024]{1,0:T(8,128)(2,1)S(1)}, u32[]{:S(2)}, u32[]{:S(2)}) collective-permute-start(bf16[512,1024]{1,0:T(8,128)(2,1)S(1)} %fusion.44), channel_id=1, source_target_pairs={{0,2},{2,0},{4,6},{6,4},{8,10},{10,8},{12,14},{14,12},{16,18},{18,... | collective-permute-start | bytes 3145736 | tf_op jit(solution)/shard_map/ppermute | solution.py:313
  658.7 51.2 %collective-permute-start.27 = (bf16[8,64,1536]{2,1,0:T(8,128)(2,1)S(1)}, bf16[8,64,1536]{2,1,0:T(8,128)(2,1)S(1)}, u32[]{:S(2)}, u32[]{:S(2)}) collective-permute-start(bf16[8,64,1536]{2,1,0:T(8,128)(2,1)S(1)} %bitcast.176), channel_id=1, source_target_pairs={{0,4},{2,6},{4,0},{6,2},{8,12},{10,14},{12,8},{14,10},{16,20},{18,... | collective-permute-start | bytes 4718600 | tf_op jit(solution)/shard_map/ppermute | solution.py:313
  661.3 45.0 %collective-permute-start.37 = (bf16[16,64,512]{2,1,0:T(8,128)(2,1)S(1)}, bf16[16,64,512]{2,1,0:T(8,128)(2,1)S(1)}, u32[]{:S(2)}, u32[]{:S(2)}) collective-permute-start(bf16[16,64,512]{2,1,0:T(8,128)(2,1)S(1)} %bitcast.190), channel_id=1, source_target_pairs={{0,0},{1,2},{2,1},{3,3},{4,4},{5,6},{6,5},{7,7},{8,8},{9,10},{10,9... | collective-permute-start | bytes 3145736 | tf_op jit(solution)/shard_map/ppermute | solution.py:305
  664.6 51.3 %collective-permute-start.48 = (bf16[8,64,2048]{2,1,0:T(8,128)(2,1)S(1)}, bf16[8,64,2048]{2,1,0:T(8,128)(2,1)S(1)}, u32[]{:S(2)}, u32[]{:S(2)}) collective-permute-start(bf16[8,64,2048]{2,1,0:T(8,128)(2,1)S(1)} %fusion.7), channel_id=1, source_target_pairs={{0,0},{1,2},{2,1},{3,3},{4,4},{5,6},{6,5},{7,7},{8,8},{9,10},{10,9... | collective-permute-start | bytes 6291464 | tf_op jit(solution)/shard_map/ppermute | solution.py:305
  668.1 32.8 %collective-permute-start.32 = (f32[4096]{0:T(1024)S(1)}, f32[4096]{0:T(1024)S(1)}, u32[]{:S(2)}, u32[]{:S(2)}) collective-permute-start(f32[4096]{0:T(1024)S(1)} %pad_maximum_fusion.10), channel_id=1, source_target_pairs={{0,1},{1,0},{2,3},{3,2},{4,5},{5,4},{6,7},{7,6},{8,9},{9,8},{10,11... | collective-permute-start | bytes 49160 | tf_op jit(solution)/shard_map/ppermute | solution.py:637
  673.0 43.7 %collective-permute-start.53 = (bf16[8,64,2048]{2,1,0:T(8,128)(2,1)S(1)}, bf16[8,64,2048]{2,1,0:T(8,128)(2,1)S(1)}, u32[]{:S(2)}, u32[]{:S(2)}) collective-permute-start(bf16[8,64,2048]{2,1,0:T(8,128)(2,1)S(1)} %get-tuple-element.45), channel_id=1, source_target_pairs={{0,2},{2,0},{4,6},{6,4},{8,10},{10,8},{12,14},{14,12},{16,18},{18,... | collective-permute-start | bytes 6291464 | tf_op jit(solution)/shard_map/ppermute | solution.py:313
  706.4 8.6 %collective-permute-start.38 = (bf16[8,64,512]{2,1,0:T(8,128)(2,1)S(1)}, bf16[8,64,512]{2,1,0:T(8,128)(2,1)S(1)}, u32[]{:S(2)}, u32[]{:S(2)}) collective-permute-start(bf16[8,64,512]{2,1,0:T(8,128)(2,1)S(1)} %get-tuple-element.63), channel_id=1, source_target_pairs={{0,2},{2,0},{4,6},{6,4},{8,10},{10,8},{12,14},{14,12},{16,18},{18,... | collective-permute-start | bytes 1572872 | tf_op jit(solution)/shard_map/ppermute | solution.py:313
  709.6 4.7 collective-permute-start.36
  710.5 19.5 %collective-permute-start.28 = (bf16[8,64,1536]{2,1,0:T(8,128)(2,1)S(1)}, bf16[8,64,1536]{2,1,0:T(8,128)(2,1)S(1)}, u32[]{:S(2)}, u32[]{:S(2)}) collective-permute-start(bf16[8,64,1536]{2,1,0:T(8,128)(2,1)S(1)} %fusion.8), channel_id=1, source_target_pairs={{0,0},{1,2},{2,1},{3,3},{4,4},{5,6},{6,5},{7,7},{8,8},{9,10},{10,9... | collective-permute-start | bytes 4718600 | tf_op jit(solution)/shard_map/ppermute | solution.py:305
  714.3 33.8 %collective-permute-start.26 = (bf16[512,1024]{1,0:T(8,128)(2,1)S(1)}, bf16[512,1024]{1,0:T(8,128)(2,1)S(1)}, u32[]{:S(2)}, u32[]{:S(2)}) collective-permute-start(bf16[512,1024]{1,0:T(8,128)(2,1)S(1)} %fusion.21), channel_id=1, source_target_pairs={{0,0},{1,2},{2,1},{3,3},{4,4},{5,6},{6,5},{7,7},{8,8},{9,10},{10,9... | collective-permute-start | bytes 3145736 | tf_op jit(solution)/shard_map/ppermute | solution.py:305
  715.2 9.2 %collective-permute-start.39 = (bf16[4,64,512]{2,1,0:T(8,128)(2,1)S(1)}, bf16[4,64,512]{2,1,0:T(8,128)(2,1)S(1)}, u32[]{:S(2)}, u32[]{:S(2)}) collective-permute-start(bf16[4,64,512]{2,1,0:T(8,128)(2,1)S(1)} %get-tuple-element.61), channel_id=1, source_target_pairs={{0,4},{2,6},{4,0},{6,2},{8,12},{10,14},{12,8},{14,10},{16,20},{18,... | collective-permute-start | bytes 786440 | tf_op jit(solution)/shard_map/ppermute | solution.py:313
  716.1 14.5 %collective-permute-start.49 = (bf16[4,64,2048]{2,1,0:T(8,128)(2,1)S(1)}, bf16[4,64,2048]{2,1,0:T(8,128)(2,1)S(1)}, u32[]{:S(2)}, u32[]{:S(2)}) collective-permute-start(bf16[4,64,2048]{2,1,0:T(8,128)(2,1)S(1)} %get-tuple-element.53), channel_id=1, source_target_pairs={{0,2},{2,0},{4,6},{6,4},{8,10},{10,8},{12,14},{14,12},{16,18},{18,... | collective-permute-start | bytes 3145736 | tf_op jit(solution)/shard_map/ppermute | solution.py:313
  717.5 29.3 %collective-permute-start.54 = (bf16[4,64,2048]{2,1,0:T(8,128)(2,1)S(1)}, bf16[4,64,2048]{2,1,0:T(8,128)(2,1)S(1)}, u32[]{:S(2)}, u32[]{:S(2)}) collective-permute-start(bf16[4,64,2048]{2,1,0:T(8,128)(2,1)S(1)} %get-tuple-element.43), channel_id=1, source_target_pairs={{0,4},{2,6},{4,0},{6,2},{8,12},{10,14},{12,8},{14,10},{16,20},{18,... | collective-permute-start | bytes 3145736 | tf_op jit(solution)/shard_map/ppermute | solution.py:313
  724.5 5.3 collective-permute-start.40
  729.9 17.5 %collective-permute-start.41 = (bf16[1,64,512]{2,1,0:T(8,128)(2,1)S(1)}, bf16[1,64,512]{2,1,0:T(8,128)(2,1)S(1)}, u32[]{:S(2)}, u32[]{:S(2)}) collective-permute-start(bf16[1,64,512]{2,1,0:T(8,128)(2,1)S(1)} %fusion.70), channel_id=1, source_target_pairs={{0,16},{2,18},{4,20},{6,22},{8,24},{10,26},{12,28},{14,30},{16,0},... | collective-permute-start | bytes 196616 | tf_op jit(solution)/shard_map/ppermute | solution.py:313
  730.1 36.5 %collective-permute-start.29 = (bf16[4,64,1536]{2,1,0:T(8,128)(2,1)S(1)}, bf16[4,64,1536]{2,1,0:T(8,128)(2,1)S(1)}, u32[]{:S(2)}, u32[]{:S(2)}) collective-permute-start(bf16[4,64,1536]{2,1,0:T(8,128)(2,1)S(1)} %get-tuple-element.58), channel_id=1, source_target_pairs={{0,2},{2,0},{4,6},{6,4},{8,10},{10,8},{12,14},{14,12},{16,18},{18,... | collective-permute-start | bytes 2359304 | tf_op jit(solution)/shard_map/ppermute | solution.py:313
  731.0 17.3 %collective-permute-start.50 = (bf16[2,64,2048]{2,1,0:T(8,128)(2,1)S(1)}, bf16[2,64,2048]{2,1,0:T(8,128)(2,1)S(1)}, u32[]{:S(2)}, u32[]{:S(2)}) collective-permute-start(bf16[2,64,2048]{2,1,0:T(8,128)(2,1)S(1)} %get-tuple-element.51), channel_id=1, source_target_pairs={{0,8},{2,10},{4,12},{6,14},{8,0},{10,2},{12,4},{14,6},{16,24},{18,... | collective-permute-start | bytes 1572872 | tf_op jit(solution)/shard_map/ppermute | solution.py:313
  746.9 19.5 %collective-permute-start.55 = (bf16[2,64,2048]{2,1,0:T(8,128)(2,1)S(1)}, bf16[2,64,2048]{2,1,0:T(8,128)(2,1)S(1)}, u32[]{:S(2)}, u32[]{:S(2)}) collective-permute-start(bf16[2,64,2048]{2,1,0:T(8,128)(2,1)S(1)} %fusion.56), channel_id=1, source_target_pairs={{0,8},{2,10},{4,12},{6,14},{8,0},{10,2},{12,4},{14,6},{16,24},{18,... | collective-permute-start | bytes 1572872 | tf_op jit(solution)/shard_map/ppermute | solution.py:313
  748.3 18.6 %collective-permute-start.51 = (bf16[1,64,2048]{2,1,0:T(8,128)(2,1)S(1)}, bf16[1,64,2048]{2,1,0:T(8,128)(2,1)S(1)}, u32[]{:S(2)}, u32[]{:S(2)}) collective-permute-start(bf16[1,64,2048]{2,1,0:T(8,128)(2,1)S(1)} %fusion.59), channel_id=1, source_target_pairs={{0,16},{2,18},{4,20},{6,22},{8,24},{10,26},{12,28},{14,30},{16,0},... | collective-permute-start | bytes 786440 | tf_op jit(solution)/shard_map/ppermute | solution.py:313
  766.5 16.4 %collective-permute-start.56 = (bf16[1,64,2048]{2,1,0:T(8,128)(2,1)S(1)}, bf16[1,64,2048]{2,1,0:T(8,128)(2,1)S(1)}, u32[]{:S(2)}, u32[]{:S(2)}) collective-permute-start(bf16[1,64,2048]{2,1,0:T(8,128)(2,1)S(1)} %fusion.57), channel_id=1, source_target_pairs={{0,16},{2,18},{4,20},{6,22},{8,24},{10,26},{12,28},{14,30},{16,0},... | collective-permute-start | bytes 786440 | tf_op jit(solution)/shard_map/ppermute | solution.py:313
  766.9 15.8 %collective-permute-start.30 = (bf16[2,64,1536]{2,1,0:T(8,128)(2,1)S(1)}, bf16[2,64,1536]{2,1,0:T(8,128)(2,1)S(1)}, u32[]{:S(2)}, u32[]{:S(2)}) collective-permute-start(bf16[2,64,1536]{2,1,0:T(8,128)(2,1)S(1)} %get-tuple-element.56), channel_id=1, source_target_pairs={{0,8},{2,10},{4,12},{6,14},{8,0},{10,2},{12,4},{14,6},{16,24},{18,... | collective-permute-start | bytes 1179656 | tf_op jit(solution)/shard_map/ppermute | solution.py:313
  782.7 10.0 %collective-permute-start.31 = (bf16[1,64,1536]{2,1,0:T(8,128)(2,1)S(1)}, bf16[1,64,1536]{2,1,0:T(8,128)(2,1)S(1)}, u32[]{:S(2)}, u32[]{:S(2)}) collective-permute-start(bf16[1,64,1536]{2,1,0:T(8,128)(2,1)S(1)} %fusion.66), channel_id=1, source_target_pairs={{0,16},{2,18},{4,20},{6,22},{8,24},{10,26},{12,28},{14,30},{16,0},... | collective-permute-start | bytes 589832 | tf_op jit(solution)/shard_map/ppermute | solution.py:313
  (37 other events, 433.6 us)
